TPU v7x, 256 devices: a whole 4x4x8 slice. The times are simulated.
256 devices in a mesh: section: 16 (over z_lo, y, core), peer: 16 (over z_hi, x).
Axes of the slice: x: 4, y: 4, z: 8 (z_hi: 4, z_lo: 2; z = z_hi * 2 + z_lo), core: 2. Of those that a mesh axis runs over, the one named last changes fastest.
Arguments:
- forward_inputs: bfloat16 [16, 16, 8, 16, 5120], P('section', 'peer'), may hold values from -6 to 6
- saved_inputs: bfloat16 [16, 16, 8, 16, 5120], P('section', 'peer'), may hold values from -6 to 6
- cotangents: bfloat16 [16, 16, 8, 16, 5120], P('section', 'peer'), may hold values from -6 to 6
- lengths: int32 [16, 16, 8], P('section', 'peer'), may hold values from 1 to 16, 80 in all within a row
- peer_counts: int32 [16], replicated, may hold values from 8 to 16, as said below
- wiring: int32 [16, 16, 8], P('section', 'peer'), may hold values from 0 to 15, as said below
- back_wiring: int32 [16, 16, 8], P('section', 'peer'), may hold values from 0 to 15, as said below
- norm_gains: float32 [16, 2, 5120], P('section'), may hold values from 0.5 to 2
- in_weights: bfloat16 [16, 2, 5120, 256], P('section', None, 'peer'), may hold values from -0.078125 to 0.078125
- down_weights: bfloat16 [16, 2, 128, 5120], P('section', None, None, 'peer'), may hold values from -0.5 to 0.5
Outputs:
- forward_arrivals: bfloat16 [16, 16, 16, 16, 5120], P('section', 'peer')
- backward_arrivals: bfloat16 [16, 16, 16, 16, 5120], P('section', 'peer')
- grad_in: float32 [16, 2, 5120, 256], P('section', None, 'peer')
- grad_down: float32 [16, 2, 128, 5120], P('section', None, None, 'peer')
Inputs may be any that keep to these rules, and one draw needn't show every extreme that they name: `peer_counts`: each section has its active peers first along peer; some section has 16 and some has 8. `wiring`: the 8 entries of one device are distinct active peers of the next section (of section 0 after the last section). `back_wiring`: the 8 entries of one device are distinct active peers of the previous section (of the last section before section 0).
All inputs are finite; a program needn't handle non-finite values.
Results may differ from a plain program's by a relative error of at most 0.02.
Values may be sent and summed in bfloat16 or wider, within the bound.
No kernel may reach another device: no remote copies, remote signals or barrier semaphores. Data moves between devices by JAX's collectives and lax.ppermute only.
A program may use at most 128 MiB of HBM per device.

v0:
```python
import jax
import jax.numpy as jnp
from jax import lax
from jax.sharding import PartitionSpec as P

EPS = 1e-05


def shifted(array, axis, by):
    count = lax.axis_size(axis)
    pairs = [(i, i + by) for i in range(count) if 0 <= i + by < count]
    return lax.ppermute(array, axis, pairs)


def contract_rows(left, right):
    return lax.dot_general(
        left, right, (((0,), (0,)), ((), ())), preferred_element_type=jnp.float32
    )


def contract_cols(left, right):
    return lax.dot_general(
        left, right, (((1,), (1,)), ((), ())), preferred_element_type=jnp.float32
    )


def layer_forward(stream, gain, weight_in, weight_down):
    inverse = lax.rsqrt(jnp.mean(stream * stream, axis=-1, keepdims=True) + EPS)
    normed = stream * inverse
    scaled = (normed * gain).astype(jnp.bfloat16)
    projected = jnp.dot(scaled, weight_in, preferred_element_type=jnp.float32)
    width = weight_down.shape[0]
    upward = projected[:, :width]
    gating = projected[:, width:]
    hidden = (jax.nn.silu(gating) * upward).astype(jnp.bfloat16)
    stream_next = stream + jnp.dot(hidden, weight_down, preferred_element_type=jnp.float32)
    return (stream_next, (inverse, normed, scaled, upward, gating, hidden))


def layer_backward(cotangent, gain, weight_in, weight_down, saved):
    inverse, normed, scaled, upward, gating, hidden = saved
    cot_low = cotangent.astype(jnp.bfloat16)
    d_hidden = contract_cols(cot_low, weight_down)
    sigmoid = jax.nn.sigmoid(gating)
    d_upward = d_hidden * (gating * sigmoid)
    d_gating = d_hidden * upward * sigmoid * (1.0 + gating * (1.0 - sigmoid))
    d_projected = jnp.concatenate([d_upward, d_gating], axis=-1).astype(jnp.bfloat16)
    d_normed = contract_cols(d_projected, weight_in) * gain
    inner = jnp.mean(d_normed * normed, axis=-1, keepdims=True)
    d_stream = cotangent + inverse * (d_normed - normed * inner)
    return (d_stream, cot_low, d_projected)


def section_forward(rows, gains, weights_in, weights_down):
    stream = rows.astype(jnp.float32)
    for depth in range(2):
        stream, unused = layer_forward(stream, gains[depth], weights_in[depth], weights_down[depth])
    return stream.astype(jnp.bfloat16)


def section_backward(rows, cotangent, gains, weights_in, weights_down):
    stream = rows.astype(jnp.float32)
    kept = []
    for depth in range(2):
        stream, saved = layer_forward(stream, gains[depth], weights_in[depth], weights_down[depth])
        kept.append(saved)
    scaled_list, cot_list, dproj_list, hidden_list = (
        [None, None],
        [None, None],
        [None, None],
        [None, None],
    )
    for depth in (1, 0):
        cotangent, cot_low, d_projected = layer_backward(
            cotangent, gains[depth], weights_in[depth], weights_down[depth], kept[depth]
        )
        scaled_list[depth] = kept[depth][2]
        hidden_list[depth] = kept[depth][5]
        cot_list[depth] = cot_low
        dproj_list[depth] = d_projected
    return (
        cotangent.astype(jnp.bfloat16),
        jnp.stack(scaled_list),
        jnp.stack(cot_list),
        jnp.stack(dproj_list),
        jnp.stack(hidden_list),
    )


def route_table(targets_local, active, peer_total):
    column = jnp.arange(peer_total, dtype=jnp.int32)
    return ((targets_local[:, None] == column[None, :]) & active).astype(jnp.bfloat16)


def per_device(
    forward_inputs,
    saved_inputs,
    cotangents,
    lengths,
    peer_counts,
    wiring,
    back_wiring,
    norm_gains,
    in_weights,
    down_weights,
):
    section_id = lax.axis_index("section")
    peer_id = lax.axis_index("peer")
    peer_total = lax.axis_size("peer")
    active = peer_id < peer_counts[section_id]
    micro = forward_inputs.shape[2]
    slots = forward_inputs.shape[3]
    width = forward_inputs.shape[4]
    full_in, full_down = (
        lax.all_gather(in_weights, "peer", axis=2, tiled=True),
        lax.all_gather(down_weights, "peer", axis=3, tiled=True),
    )
    gains = norm_gains[0]
    weights_in = full_in[0]
    weights_down = full_down[0]
    outputs = section_forward(
        forward_inputs.reshape(micro * slots, width), gains, weights_in, weights_down
    )
    outputs = outputs.reshape(micro, slots, width)
    routing = route_table(wiring[0, 0], active, peer_total)
    outgoing = jnp.einsum(
        "mq,mtd->qtd", routing, outputs, preferred_element_type=jnp.float32
    ).astype(jnp.bfloat16)
    positions = jnp.arange(slots, dtype=jnp.int32)
    live = ((positions[None, :] < lengths[0, 0][:, None]) & active).astype(jnp.float32)
    cotangent = cotangents[0, 0].astype(jnp.float32) * live[:, :, None]
    d_rows, scaled_all, cot_all, dproj_all, hidden_all = section_backward(
        saved_inputs.reshape(micro * slots, width),
        cotangent.reshape(micro * slots, width),
        gains,
        weights_in,
        weights_down,
    )
    d_rows = d_rows.reshape(micro, slots, width)
    back_routing = route_table(back_wiring[0, 0], active, peer_total)
    back_outgoing = jnp.einsum(
        "mq,mtd->qtd", back_routing, d_rows, preferred_element_type=jnp.float32
    ).astype(jnp.bfloat16)
    received = lax.all_to_all(outgoing, "peer", split_axis=0, concat_axis=0, tiled=True)
    forward_arrived = shifted(received, "section", 1)
    back_received = lax.all_to_all(back_outgoing, "peer", split_axis=0, concat_axis=0, tiled=True)
    backward_arrived = shifted(back_received, "section", -1)
    grad_in_part = jnp.stack(
        [contract_rows(scaled_all[depth], dproj_all[depth]) for depth in range(2)]
    )
    grad_down_part = jnp.stack(
        [contract_rows(hidden_all[depth], cot_all[depth]) for depth in range(2)]
    )
    grad_in, grad_down = (
        lax.psum_scatter(
            grad_in_part.astype(jnp.bfloat16), "peer", scatter_dimension=1, tiled=True
        ).astype(jnp.float32),
        lax.psum_scatter(
            grad_down_part.astype(jnp.bfloat16), "peer", scatter_dimension=2, tiled=True
        ).astype(jnp.float32),
    )
    forward_arrivals = forward_arrived.reshape(1, 1, peer_total, slots, width)
    backward_arrivals = backward_arrived.reshape(1, 1, peer_total, slots, width)
    return (forward_arrivals, backward_arrivals, grad_in[None], grad_down[None])


def solution(mesh):
    return jax.shard_map(
        per_device,
        mesh=mesh,
        in_specs=(
            P("section", "peer", None, None, None),
            P("section", "peer", None, None, None),
            P("section", "peer", None, None, None),
            P("section", "peer", None),
            P(),
            P("section", "peer", None),
            P("section", "peer", None),
            P("section", None, None),
            P("section", None, "peer", None),
            P("section", None, None, "peer"),
        ),
        out_specs=(
            P("section", "peer", None, None, None),
            P("section", "peer", None, None, None),
            P("section", None, "peer", None),
            P("section", None, None, "peer"),
        ),
        check_vma=False,
    )
```

profile of v0, /device:TPU:25, one launch (start us, length us, event | category | flops | bytes accessed | tf_op | source)
XLA Modules:
  0.0 576.6 jit_solution(3579577942034423740)
XLA Ops:
  7.2 0.0 all-gather.3.cloned.1.call-start
  7.2 0.7 all-gather.3.cloned.1.call-update
  7.9 0.0 all-gather.5.cloned.1.call-start
  8.0 0.7 all-gather.5.cloned.1.call-update
  8.7 0.0 all-reduce.3.cloned.1.call-start
  8.7 1.2 dynamic_slice.3
  10.6 0.7 fusion.34
  11.4 0.1 reshape.171
  11.4 1.7 multiply_reduce_fusion.3
  13.2 0.3 multiply_reduce_fusion.5
  13.6 1.4 multiply_convert_fusion.2
  15.0 1.8 multiply_convert_fusion.3
  16.8 84.4 %all-gather.3.cloned.1.call-done = bf16[1,2,5120,256]{3,2,1,0:T(8,128)(2,1)} async-done(((bf16[1,2,320,256]{3,2,1,0:T(8,128)(2,1)}), bf16[1,2,5120,256]{3,2,1,0:T(8,128)(2,1)}) %all-gather.3.cloned.1.call-update) | async-done | bytes 5242896 | tf_op jit(solution)/shard_map/all_gather | solution.py:115
  101.2 2.7 fusion.7
  103.9 61.1 %all-gather.5.cloned.1.call-done = bf16[1,2,128,5120]{2,3,1,0:T(8,128)(2,1)} async-done(((bf16[1,2,128,320]{2,3,1,0:T(8,128)(2,1)}), bf16[1,2,128,5120]{2,3,1,0:T(8,128)(2,1)}) %all-gather.5.cloned.1.call-update) | async-done | bytes 2621456 | tf_op jit(solution)/shard_map/all_gather | solution.py:116
  165.0 3.5 multiply_reduce_fusion.4
  168.5 0.5 fusion.6
  169.1 0.7 copy-done.3
  169.8 0.8 copy-done.8
  170.6 0.6 multiply_reduce_fusion.2
  171.2 0.6 fusion.8
  171.8 0.7 copy-done.12
  172.5 0.5 multiply_convert_fusion.11
  173.1 1.1 multiply_reduce_fusion.1
  174.2 0.2 copy-done.11
  174.4 0.9 fusion.5
  175.3 0.5 fusion.4
  175.9 0.5 fusion.3
  176.4 0.4 copy-done
  176.8 1.8 pad_maximum_fusion.1
  178.6 7.4 %copy.31 = bf16[2,128,5120]{1,0,2:T(2,128)(2,1)} copy(bf16[2,128,5120]{2,1,0:T(8,128)(2,1)} %pad_maximum_fusion.1) | data formatting | bytes 5242880 | tf_op jit(solution)/shard_map/stack | solution.py:151
  186.0 0.0 all-reduce.3.cloned.1.call-update
  186.1 3.2 fusion.9
  189.3 0.0 copy-done.5
  189.3 0.8 copy-done.9
  190.1 0.5 fusion.2
  190.7 0.1 copy-done.14
  190.8 1.4 convolution_convert_fusion.3
  192.2 2.9 copy.24
  195.2 6.0 %all-to-all-start = ((bf16[16,16,5120]{2,1,0:T(8,128)(2,1)}), bf16[16,16,5120]{2,1,0:T(8,128)(2,1)}, u32[]{:S(2)}, u32[]{:S(2)}) async-start(bf16[16,16,5120]{2,1,0:T(8,128)(2,1)} %copy.24), calls=%async_computation | async-start | bytes 5242880 | tf_op jit(solution)/shard_map/all_to_all | solution.py:144
  201.1 0.2 reduce-scatter.2.cloned.1.call-start
  201.4 0.1 rsqrt.40
  201.4 2.7 multiply_convert_fusion.9
  204.2 4.3 multiply_convert_fusion
  208.5 0.9 fusion
  209.3 1.0 fusion.1
  210.3 2.8 pad_maximum_fusion
  213.1 1.7 copy-done.1
  214.8 2.9 add_convert_fusion
  217.7 1.4 convolution_convert_fusion.2
  219.2 2.9 copy.30
  222.1 52.4 %all-to-all-done = bf16[16,16,5120]{2,1,0:T(8,128)(2,1)} async-done(((bf16[16,16,5120]{2,1,0:T(8,128)(2,1)}), bf16[16,16,5120]{2,1,0:T(8,128)(2,1)}, u32[]{:S(2)}, u32[]{:S(2)}) %all-to-all-start) | async-done | bytes 2621472 | tf_op jit(solution)/shard_map/all_to_all | solution.py:144
  274.5 16.1 %all-to-all-start.1 = ((bf16[16,16,5120]{2,1,0:T(8,128)(2,1)}), bf16[16,16,5120]{2,1,0:T(8,128)(2,1)}, u32[]{:S(2)}, u32[]{:S(2)}) async-start(bf16[16,16,5120]{2,1,0:T(8,128)(2,1)} %copy.30), calls=%async_computation.1 | async-start | bytes 5242880 | tf_op jit(solution)/shard_map/all_to_all | solution.py:146
  290.7 9.0 %collective-permute-start = (bf16[16,16,5120]{2,1,0:T(8,128)(2,1)}, bf16[16,16,5120]{2,1,0:T(8,128)(2,1)S(1)}, u32[]{:S(2)}, u32[]{:S(2)}) collective-permute-start(bf16[16,16,5120]{2,1,0:T(8,128)(2,1)} %all-to-all-done), channel_id=1, source_target_pairs={{0,16},{16,32},{32,48},{48,64},{64,80},{80,96},{96,112},{112,128},... | collective-permute-start | bytes 7864328 | tf_op jit(solution)/shard_map/ppermute | solution.py:12
  299.6 59.7 %all-to-all-done.1 = bf16[16,16,5120]{2,1,0:T(8,128)(2,1)} async-done(((bf16[16,16,5120]{2,1,0:T(8,128)(2,1)}), bf16[16,16,5120]{2,1,0:T(8,128)(2,1)}, u32[]{:S(2)}, u32[]{:S(2)}) %all-to-all-start.1) | async-done | bytes 2621472 | tf_op jit(solution)/shard_map/all_to_all | solution.py:146
  359.4 5.5 collective-permute-start.1
  364.9 0.6 dynamic-slice
  366.1 91.9 %all-reduce.3.cloned.1.call-done = bf16[2,128,5120]{1,0,2:T(2,128)(2,1)} async-done(((bf16[2,128,5120]{1,0,2:T(2,128)(2,1)}), bf16[2,128,5120]{1,0,2:T(2,128)(2,1)}) %all-reduce.3.cloned.1.call-update) | async-done | bytes 2621456
  458.1 1.0 bitcast_convert_fusion.1
  459.1 0.7 copy.32
  459.8 103.4 %reduce-scatter.2.cloned.1.call-done = bf16[2,320,256]{2,1,0:T(8,128)(2,1)} async-done(((bf16[2,5120,256]{2,1,0:T(8,128)(2,1)}), bf16[2,320,256]{2,1,0:T(8,128)(2,1)}) %reduce-scatter.2.cloned.1.call-update) | async-done | bytes 327696 | tf_op jit(solution)/shard_map/reduce_scatter | solution.py:155
  563.2 1.9 bitcast_convert_fusion
  565.1 1.5 copy.42
  566.6 3.5 copy.43
  (36 shorter events, 0.2 us)
Async XLA Ops:
  7.2 6.0 %copy-start.7 = (bf16[1,1,8,16,5120]{4,3,2,1,0:T(8,128)(2,1)S(1)}, bf16[1,1,8,16,5120]{4,3,2,1,0:T(8,128)(2,1)}, u32[]{:S(2)}) copy-start(bf16[1,1,8,16,5120]{4,3,2,1,0:T(8,128)(2,1)} %param.10) | copy-start | bytes 3932164
  7.2 6.4 %copy-start.13 = (f32[1,2,5120]{2,1,0:T(2,128)S(1)}, f32[1,2,5120]{2,1,0:T(2,128)}, u32[]{:S(2)}) copy-start(f32[1,2,5120]{2,1,0:T(2,128)} %param.17) | copy-start | bytes 122884
  7.2 6.4 %copy-start.10 = (bf16[1,1,8,16,5120]{4,3,2,1,0:T(8,128)(2,1)S(1)}, bf16[1,1,8,16,5120]{4,3,2,1,0:T(8,128)(2,1)}, u32[]{:S(2)}) copy-start(bf16[1,1,8,16,5120]{4,3,2,1,0:T(8,128)(2,1)} %param.12) | copy-start | bytes 3932164
  7.2 94.0 %all-gather.3.cloned.1.call-start = ((), (), s32[]{:S(2)}) async-start(), calls=%async_computation.3 | async-start | bytes 5570560 | tf_op jit(solution)/shard_map/all_gather | solution.py:115
  7.9 157.1 %all-gather.5.cloned.1.call-start = ((), (), s32[]{:S(2)}) async-start(), calls=%async_computation.4 | async-start | bytes 2785280 | tf_op jit(solution)/shard_map/all_gather | solution.py:116
  8.7 449.4 %all-reduce.3.cloned.1.call-start = ((), (), s32[]{:S(2)}) async-start(), calls=%async_computation.6 | async-start | bytes 5242880
  11.4 3.6 copy-start.2
  165.0 3.5 copy-start.6
  168.5 1.3 copy-start.3
  168.5 2.1 copy-start.8
  171.2 1.3 copy-start.12
  173.1 1.3 copy-start.11
  175.3 1.5 copy-start
  186.0 3.3 copy-start.5
  186.1 4.1 copy-start.9
  190.1 0.7 copy-start.14
  195.2 79.3 %all-to-all-start = ((bf16[16,16,5120]{2,1,0:T(8,128)(2,1)}), bf16[16,16,5120]{2,1,0:T(8,128)(2,1)}, u32[]{:S(2)}, u32[]{:S(2)}) async-start(bf16[16,16,5120]{2,1,0:T(8,128)(2,1)} %copy.24), calls=%async_computation | async-start | bytes 5242880 | tf_op jit(solution)/shard_map/all_to_all | solution.py:144
  201.1 362.1 %reduce-scatter.2.cloned.1.call-start = ((), (), s32[]{:S(2)}) async-start(), calls=%async_computation.5 | async-start | bytes 5570560 | tf_op jit(solution)/shard_map/reduce_scatter | solution.py:155
  201.4 2.7 copy-start.4
  213.1 1.8 copy-start.1
  214.8 2.9 copy-start.15
  222.1 142.8 %copy-start.16 = (u32[256]{0:T(256)S(1)}, u32[256]{0:T(256)}, u32[]{:S(2)}) copy-start(u32[256]{0:T(256)} %constant.41) | copy-start | bytes 3076
  274.5 84.9 %all-to-all-start.1 = ((bf16[16,16,5120]{2,1,0:T(8,128)(2,1)}), bf16[16,16,5120]{2,1,0:T(8,128)(2,1)}, u32[]{:S(2)}, u32[]{:S(2)}) async-start(bf16[16,16,5120]{2,1,0:T(8,128)(2,1)} %copy.30), calls=%async_computation.1 | async-start | bytes 5242880 | tf_op jit(solution)/shard_map/all_to_all | solution.py:146
  290.7 169.2 %collective-permute-start = (bf16[16,16,5120]{2,1,0:T(8,128)(2,1)}, bf16[16,16,5120]{2,1,0:T(8,128)(2,1)S(1)}, u32[]{:S(2)}, u32[]{:S(2)}) collective-permute-start(bf16[16,16,5120]{2,1,0:T(8,128)(2,1)} %all-to-all-done), channel_id=1, source_target_pairs={{0,16},{16,32},{32,48},{48,64},{64,80},{80,96},{96,112},{112,128},... | collective-permute-start | bytes 7864328 | tf_op jit(solution)/shard_map/ppermute | solution.py:12
  359.4 100.4 %collective-permute-start.1 = (bf16[16,16,5120]{2,1,0:T(8,128)(2,1)}, bf16[16,16,5120]{2,1,0:T(8,128)(2,1)}, u32[]{:S(2)}, u32[]{:S(2)}) collective-permute-start(bf16[16,16,5120]{2,1,0:T(8,128)(2,1)} %all-to-all-done.1), channel_id=1, source_target_pairs={{16,0},{32,16},{48,32},{64,48},{80,64},{96,80},{112,96},{128,112},... | collective-permute-start | bytes 7864328 | tf_op jit(solution)/shard_map/ppermute | solution.py:12
Sparse Core Ops, SparseCore 0:
  10.5 90.6 all-gather.2
  103.6 61.3 all-gather.4
  186.2 271.8 all-reduce.2
  461.6 101.6 reduce-scatter.1
where the time goes:
time: 578 us; the launch traced here: 577 us
  waiting for transfers between devices  454 us (79%)
  starting transfers between devices  36.9 us (6%)
  local copies, waits for them, and re-layouts  26.6 us (5%)
  matrix products  26 us (4%)
  other arithmetic  17.3 us (3%)
  between operations  15.4 us (3%)
    reduce_scatter x1, waiting for transfers between devices, per_device(): lax.psum_scatter(grad_in_part.astype(jnp.bfloat16), 'peer', scatter_dimen...  103 us
    unnamed x5, waiting for transfers between devices  93.3 us
    all_gather x1, waiting for transfers between devices, per_device(): lax.all_gather(in_weights, 'peer', axis=2, tiled=True)  84.4 us
    all_gather x1, waiting for transfers between devices, per_device(): lax.all_gather(down_weights, 'peer', axis=3, tiled=True)  61.1 us
    all_to_all x1, waiting for transfers between devices, per_device(): lax.all_to_all(back_outgoing, 'peer', split_axis=0, concat_axis=0, tiled=...  59.7 us
    all_to_all x1, waiting for transfers between devices, per_device(): lax.all_to_all(outgoing, 'peer', split_axis=0, concat_axis=0, tiled=True)  52.4 us
    all_to_all x1, starting transfers between devices, per_device(): lax.all_to_all(back_outgoing, 'peer', split_axis=0, concat_axis=0, tiled=...  16.1 us
    ppermute x2, starting transfers between devices, shifted(): return lax.ppermute(array, axis, pairs)  14.5 us
  transfers between devices with their start and end apart: 8, of which 6 were waited for; matrix products, arithmetic and copies ran while one was open for 7% of the time, Pallas kernels for 0%

commit v1 on v0

v1 whole, which is shorter than its diff:
```python
import functools

import jax
import jax.numpy as jnp
from jax import lax
from jax.experimental import pallas as pl
from jax.experimental.pallas import tpu as pltpu
from jax.sharding import PartitionSpec as P

EPS = 1e-05
CHUNK = 640
ROW = 4


def move(array, dz, dx, ds=0):
    sections, peers = lax.axis_size("section"), lax.axis_size("peer")
    rows = peers // ROW
    pairs = []
    for s in range(sections):
        if not 0 <= s + ds < sections:
            continue
        for z in range(rows):
            for x in range(ROW):
                there = ((z + dz) % rows) * ROW + (x + dx) % ROW
                pairs.append((s * peers + z * ROW + x, (s + ds) * peers + there))
    return lax.ppermute(array, ("section", "peer"), pairs)


def along(axis, by):
    return (by, 0) if axis == "z" else (0, by)


def ring_gather(block, axis):
    half = block.shape[0] // 2
    ahead = move(block, *along(axis, 1))
    behind = move(block, *along(axis, -1))
    far_low = move(ahead[:half], *along(axis, 1))
    far_high = move(behind[half:], *along(axis, -1))
    return [(0, 0, block), (-1, 0, ahead), (1, 0, behind), (2, 0, far_low), (2, half, far_high)]


OFFSETS = (0, -1, 1, 2)


def near_gather(piece, axis):
    return jnp.concatenate([piece] + [move(piece, *along(axis, -offset)) for offset in OFFSETS[1:]], axis=0)


def far_gather(lead, axis, parts):
    rows = lead.shape[0] // ROW
    held = []
    for far, row, block in ring_gather(lead, axis):
        spans = []
        for i in range(block.shape[0] // rows):
            near = OFFSETS[row // rows + i]
            dz, dx = (near, far) if axis == "x" else (far, near)
            at = i * rows
            for layer, start, count in parts:
                spans.append((at, dz, dx, layer, start, count))
                at += count
        held.append((block, spans))
    return held


def put_together(full_refs, refs, spans, where_ref, share, sems):
    copies = [[] for _ in full_refs]
    count = 0
    for ref, held in zip(refs, spans, strict=True):
        for row, dz, dx, layer, start, rows in held:
            z = lax.rem(where_ref[0] + (dz + ROW), ROW)
            x = lax.rem(where_ref[1] + (dx + ROW), ROW)
            there = pl.multiple_of((z * ROW + x) * share + start, 16)
            copy = pltpu.make_async_copy(
                ref.at[pl.ds(row, rows), :], full_refs[layer].at[pl.ds(there, rows), :], sems.at[count]
            )
            copy.start()
            copies[layer].append(copy)
            count += 1
    return copies


def wait_all(copies):
    for copy in copies:
        copy.wait()


def loop(steps, body, carry):
    for step in range(steps):
        carry = body(step, carry)
    return carry


def columns(step):
    return slice(step * CHUNK, (step + 1) * CHUNK)


def dot(left, right):
    return jnp.dot(left, right, preferred_element_type=jnp.float32)


def dot_cols(left, right):
    return lax.dot_general(left, right, (((1,), (1,)), ((), ())), preferred_element_type=jnp.float32)


def dot_rows(left, right):
    return lax.dot_general(left, right, (((0,), (0,)), ((), ())), preferred_element_type=jnp.float32)


def inverse_norm(stream_ref):
    rows, width = stream_ref.shape

    def add(step, total):
        part = stream_ref[:, columns(step)].astype(jnp.float32)
        return total + jnp.sum(part * part, axis=-1, keepdims=True)

    total = loop(width // CHUNK, add, jnp.zeros((rows, 1), jnp.float32))
    return lax.rsqrt(total / width + EPS)


def project(stream_ref, inverse, gain_ref, layer, full_ref):
    rows, width = stream_ref.shape
    rank = full_ref.shape[1] // 3

    def add(step, total):
        cols = columns(step)
        normed = stream_ref[:, cols].astype(jnp.float32) * inverse
        scaled = (normed * gain_ref[layer : layer + 1, cols]).astype(jnp.bfloat16)
        return total + dot(scaled, full_ref[cols, : 2 * rank])

    return loop(width // CHUNK, add, jnp.zeros((rows, 2 * rank), jnp.float32))


def gate(projected):
    rank = projected.shape[1] // 2
    upward, gating = projected[:, :rank], projected[:, rank:]
    sigmoid = jax.nn.sigmoid(gating)
    hidden = (gating * sigmoid * upward).astype(jnp.bfloat16)
    return upward, gating, sigmoid, hidden


def step_back(d_hidden, projected):
    upward, gating, sigmoid, hidden = gate(projected)
    d_upward = d_hidden * (gating * sigmoid)
    d_gating = d_hidden * upward * sigmoid * (1.0 + gating * (1.0 - sigmoid))
    return jnp.concatenate([d_upward, d_gating], axis=-1).astype(jnp.bfloat16), hidden


def hand_out(index_ref, rows_ref, routed_ref, slots):
    for peer in range(routed_ref.shape[0]):
        index = index_ref[peer]

        @pl.when(index >= 0)
        def _(index=index, peer=peer):
            start = pl.multiple_of(jnp.maximum(index, 0) * slots, slots)
            routed_ref[peer] = rows_ref[pl.ds(start, slots), :]

        @pl.when(index < 0)
        def _(peer=peer):
            routed_ref[peer] = jnp.zeros((slots, rows_ref.shape[1]), rows_ref.dtype)


def forward_kernel(spans, share, slots, where_ref, index_ref, gain_ref, input_ref, *refs):
    blocks = refs[: len(spans)]
    routed_ref, low_full_ref, high_full_ref, stream_ref, rows_ref, sems = refs[len(spans) :]
    copies = put_together((low_full_ref, high_full_ref), blocks, spans, where_ref, share, sems)
    rank = low_full_ref.shape[1] // 3
    steps = input_ref.shape[1] // CHUNK
    inverse = inverse_norm(input_ref)
    wait_all(copies[0])
    hidden = gate(project(input_ref, inverse, gain_ref, 0, low_full_ref))[3]

    def lower(step, total):
        cols = columns(step)
        new = input_ref[:, cols].astype(jnp.float32) + dot_cols(hidden, low_full_ref[cols, 2 * rank :])
        stream_ref[:, cols] = new
        return total + jnp.sum(new * new, axis=-1, keepdims=True)

    total = loop(steps, lower, jnp.zeros((input_ref.shape[0], 1), jnp.float32))
    inverse = lax.rsqrt(total / input_ref.shape[1] + EPS)
    wait_all(copies[1])
    hidden_high = gate(project(stream_ref, inverse, gain_ref, 1, high_full_ref))[3]

    def upper(step, carry):
        cols = columns(step)
        new = stream_ref[:, cols] + dot_cols(hidden_high, high_full_ref[cols, 2 * rank :])
        rows_ref[:, cols] = new.astype(jnp.bfloat16)
        return carry

    loop(steps, upper, 0)
    hand_out(index_ref, rows_ref, routed_ref, slots)


def spread_kernel(slots, index_ref, rows_ref, routed_ref):
    hand_out(index_ref, rows_ref, routed_ref, slots)


def back_kernel(spans, share, where_ref, gain_ref, saved_ref, cot_ref, *refs):
    blocks, refs = refs[: len(spans)], refs[len(spans) :]
    rows_ref, own_ref, up_ref, down_ref, next_ref, last_ref = refs[:6]
    low_full_ref, high_full_ref, stream_ref, scaled_ref, cot_low_ref, cot_high_ref, grad_ref, sems = refs[6:]
    copies = put_together((low_full_ref, high_full_ref), blocks, spans, where_ref, share, sems)
    count, width = saved_ref.shape
    rank = low_full_ref.shape[1] // 3
    steps = width // CHUNK
    f32, bf16 = jnp.float32, jnp.bfloat16
    nothing = jnp.zeros((count, rank), f32)

    inverse_low = inverse_norm(saved_ref)
    wait_all(copies[0])
    projected_low = project(saved_ref, inverse_low, gain_ref, 0, low_full_ref)
    hidden_low = gate(projected_low)[3]

    def first(step, total):
        cols = columns(step)
        new = saved_ref[:, cols].astype(f32) + dot_cols(hidden_low, low_full_ref[cols, 2 * rank :])
        stream_ref[:, cols] = new
        return total + jnp.sum(new * new, axis=-1, keepdims=True)

    total = loop(steps, first, jnp.zeros((count, 1), f32))
    inverse = lax.rsqrt(total / width + EPS)
    wait_all(copies[1])

    def forward(step, carry):
        projected, d_hidden = carry
        cols = columns(step)
        scaled = (stream_ref[:, cols] * inverse * gain_ref[1:2, cols]).astype(bf16)
        scaled_ref[:, cols] = scaled
        projected = projected + dot(scaled, high_full_ref[cols, : 2 * rank])
        d_hidden = d_hidden + dot(cot_ref[:, cols], high_full_ref[cols, 2 * rank :])
        return projected, d_hidden

    projected, d_hidden = loop(
        steps, forward, (jnp.zeros((count, 2 * rank), f32), nothing)
    )
    d_projected, hidden = step_back(d_hidden, projected)
    inner = jnp.sum(d_projected.astype(f32) * projected, axis=-1, keepdims=True) / width

    def store_grad(layer, step, scaled, cot_low, d_projected, hidden):
        peer = step * (CHUNK // share)
        wide = dot_rows(scaled, d_projected).astype(bf16)
        down = dot_rows(cot_low, hidden).astype(bf16)
        for i in range(CHUNK // share):
            grad_ref[layer, peer + i, :, : 2 * rank] = wide[i * share : (i + 1) * share]
            grad_ref[layer, peer + i, :, 2 * rank :] = down[i * share : (i + 1) * share]

    def upper(step, d_hidden_low):
        cols = columns(step)
        d_normed = dot_cols(d_projected, high_full_ref[cols, : 2 * rank]) * gain_ref[1:2, cols]
        normed = stream_ref[:, cols] * inverse
        cot_low = cot_ref[:, cols]
        new = cot_low.astype(f32) + inverse * (d_normed - normed * inner)
        cot_high_ref[:, cols] = new
        low = new.astype(bf16)
        cot_low_ref[:, cols] = low
        store_grad(1, step, scaled_ref[:, cols], cot_low, d_projected, hidden)
        return d_hidden_low + dot(low, low_full_ref[cols, 2 * rank :])

    d_hidden_low = loop(steps, upper, nothing)
    d_projected_low, _ = step_back(d_hidden_low, projected_low)
    inner_low = jnp.sum(d_projected_low.astype(f32) * projected_low, axis=-1, keepdims=True) / width

    def lower(step, carry):
        cols = columns(step)
        gain = gain_ref[0:1, cols]
        d_normed = dot_cols(d_projected_low, low_full_ref[cols, : 2 * rank]) * gain
        normed = saved_ref[:, cols].astype(f32) * inverse_low
        new = cot_high_ref[:, cols] + inverse_low * (d_normed - normed * inner_low)
        rows_ref[:, cols] = new.astype(bf16)
        scaled = (normed * gain).astype(bf16)
        store_grad(0, step, scaled, cot_low_ref[:, cols], d_projected_low, hidden_low)
        return carry

    loop(steps, lower, 0)

    half = share // 2
    for layer in range(2):
        for dz in range(ROW):
            z = lax.rem(where_ref[0] + dz, ROW) * ROW
            own, ahead, far, behind = (z + lax.rem(where_ref[1] + dx, ROW) for dx in range(ROW))
            own_ref[layer, dz] = grad_ref[layer, own]
            up_ref[0, layer, dz] = grad_ref[layer, far, :half]
            up_ref[1, layer, dz] = grad_ref[layer, ahead, half:]
            down_ref[0, layer, dz] = grad_ref[layer, far, half:]
            down_ref[1, layer, dz] = grad_ref[layer, behind, :half]
            next_ref[layer, dz] = grad_ref[layer, ahead, :half]
            last_ref[layer, dz] = grad_ref[layer, behind, half:]


def vmem(count):
    return [pl.BlockSpec(memory_space=pltpu.VMEM)] * count


def smem(count):
    return [pl.BlockSpec(memory_space=pltpu.SMEM)] * count


def shaped(*shape, dtype=jnp.bfloat16):
    return jax.ShapeDtypeStruct(shape, dtype)


def exchange(routed):
    return lax.all_to_all(routed, "peer", split_axis=0, concat_axis=0, tiled=True)


def slots_of(targets, active):
    names = jnp.arange(lax.axis_size("peer"), dtype=jnp.int32)
    table = (targets[:, None] == names[None, :]) & active
    micro = jnp.arange(targets.shape[0], dtype=jnp.int32)
    return jnp.max(jnp.where(table, micro[:, None], -1), axis=0)


def add_up(*terms):
    total = terms[0].astype(jnp.float32)
    for term in terms[1:]:
        total = total + term.astype(jnp.float32)
    return total


def scatter_first(up, down, axis):
    return move(up, *along(axis, 1)), move(down, *along(axis, -1))


def scatter_rest(own, ahead, behind, got_up, got_down, axis):
    half = ahead.shape[-2]
    ahead = add_up(ahead, got_up[0]).astype(own.dtype)
    behind = add_up(behind, got_down[0]).astype(own.dtype)
    ahead, behind = lax.optimization_barrier((ahead, behind))
    got_ahead, got_behind = move(ahead, *along(axis, 1)), move(behind, *along(axis, -1))
    low = add_up(own[..., :half, :], got_ahead, got_down[1])
    high = add_up(own[..., half:, :], got_behind, got_up[1])
    return low, high


def reduce_scatter(own, ahead, behind, got_up, got_down, after):
    dtype = own.dtype
    low, high = scatter_rest(own, ahead, behind, got_up, got_down, "x")
    low, high = low.astype(dtype), high.astype(dtype)
    up, down = scatter_first(
        jnp.stack([low[:, 2], high[:, 1]]), jnp.stack([high[:, 2], low[:, 3]]), "z"
    )
    mine = jnp.concatenate([low[:, 0], high[:, 0]], axis=1)
    low, high = scatter_rest(mine, low[:, 1], high[:, 3], up, down, "z")
    low, high, after = lax.optimization_barrier((low, high, after))
    return jnp.concatenate([low, high], axis=1), after


def cost(micros):
    return pl.CostEstimate(flops=micros * 10**9, bytes_accessed=micros * 3 * 10**6, transcendentals=0)


def per_device(
    forward_inputs,
    saved_inputs,
    cotangents,
    lengths,
    peer_counts,
    wiring,
    back_wiring,
    norm_gains,
    in_weights,
    down_weights,
):
    section_id = lax.axis_index("section")
    peer_id = lax.axis_index("peer")
    where = jnp.stack([peer_id // ROW, peer_id % ROW]).astype(jnp.int32)
    active = peer_id < peer_counts[section_id]
    micro, slots, width = forward_inputs.shape[2:]
    count = micro * slots
    rank = down_weights.shape[2]
    share = in_weights.shape[2]
    gains = norm_gains[0]
    f32 = jnp.float32

    both = jnp.concatenate([in_weights[0], jnp.swapaxes(down_weights[0], 1, 2)], axis=-1)
    cut = share * 45 // 100 // 16 * 16
    by_z = near_gather(jnp.concatenate([both[0], both[1, :cut]], axis=0), "z")
    by_x = near_gather(both[1, cut:], "x")
    by_z, by_x = lax.optimization_barrier((by_z, by_x))
    blocks = far_gather(by_z, "x", [(0, 0, share), (1, 0, cut)])
    blocks += far_gather(by_x, "z", [(1, cut, share - cut)])

    forward_slots = slots_of(wiring[0, 0], active)
    back_slots = move(slots_of(back_wiring[0, 0], active), 0, 0, -1)
    positions = jnp.arange(slots, dtype=jnp.int32)
    live = (positions[None, :] < lengths[0, 0][:, None]) & active
    cot = jnp.where(live[:, :, None], cotangents[0, 0], jnp.zeros((), cotangents.dtype))
    cot = cot.reshape(count, width)
    saved = saved_inputs.reshape(count, width)

    peers = ROW * ROW
    routed = shaped(peers, slots, width)
    flat = shaped(count, width)
    bf16 = jnp.bfloat16

    spans = [held for _, held in blocks]
    arrays = [array for array, _ in blocks]
    anywhere = [pl.BlockSpec(memory_space=pl.ANY)] * len(spans)
    wide = [pltpu.VMEM((width, 3 * rank), bf16)] * 2
    sems = pltpu.SemaphoreType.DMA((sum(len(held) for held in spans),))
    outgoing = pl.pallas_call(
        functools.partial(forward_kernel, spans, share, slots),
        out_shape=routed,
        in_specs=smem(2) + vmem(2) + anywhere,
        out_specs=vmem(1)[0],
        scratch_shapes=wide + [pltpu.VMEM((count, width), f32), pltpu.VMEM((count, width), bf16), sems],
        compiler_params=pltpu.CompilerParams(vmem_limit_bytes=40 << 20),
        cost_estimate=cost(12),
    )(where, forward_slots, gains, forward_inputs.reshape(count, width), *arrays)

    outgoing, saved = lax.optimization_barrier((outgoing, saved))
    forward_arrived = move(exchange(outgoing), 0, 0, 1)

    part = shaped(2, ROW, share // 2, 3 * rank)
    pair = shaped(2, 2, ROW, share // 2, 3 * rank)
    d_rows, own, up, down, ahead, behind = pl.pallas_call(
        functools.partial(back_kernel, spans, share),
        out_shape=[flat, shaped(2, ROW, share, 3 * rank), pair, pair, part, part],
        in_specs=smem(1) + vmem(3) + anywhere,
        out_specs=vmem(6),
        scratch_shapes=wide
        + [
            pltpu.VMEM((count, width), f32),
            pltpu.VMEM((count, width), bf16),
            pltpu.VMEM((count, width), bf16),
            pltpu.VMEM((count, width), f32),
            pltpu.VMEM((2, peers, share, 3 * rank), bf16),
            sems,
        ],
        compiler_params=pltpu.CompilerParams(vmem_limit_bytes=52 << 20),
        cost_estimate=cost(25),
    )(where, gains, saved, cot, *arrays)
    returned = pl.pallas_call(
        functools.partial(spread_kernel, slots),
        out_shape=routed,
        in_specs=smem(1) + vmem(1),
        out_specs=vmem(1)[0],
        compiler_params=pltpu.CompilerParams(vmem_limit_bytes=16 << 20),
        cost_estimate=cost(2),
    )(back_slots, move(d_rows, 0, 0, -1))
    got_up, got_down = scatter_first(up, down, "x")
    returned, got_up, got_down = lax.optimization_barrier((returned, got_up, got_down))
    backward_arrived = exchange(returned)
    total, forward_arrived = reduce_scatter(own, ahead, behind, got_up, got_down, forward_arrived)

    grad_in = total[:, :, : 2 * rank]
    grad_down = jnp.swapaxes(total[:, :, 2 * rank :], 1, 2)
    return (
        forward_arrived.reshape(1, 1, peers, slots, width),
        backward_arrived.reshape(1, 1, peers, slots, width),
        grad_in[None],
        grad_down[None],
    )


def solution(mesh):
    return jax.shard_map(
        per_device,
        mesh=mesh,
        in_specs=(
            P("section", "peer", None, None, None),
            P("section", "peer", None, None, None),
            P("section", "peer", None, None, None),
            P("section", "peer", None),
            P(),
            P("section", "peer", None),
            P("section", "peer", None),
            P("section", None, None),
            P("section", None, "peer", None),
            P("section", None, None, "peer"),
        ),
        out_specs=(
            P("section", "peer", None, None, None),
            P("section", "peer", None, None, None),
            P("section", None, "peer", None),
            P("section", None, None, "peer"),
        ),
        check_vma=False,
    )
```

time: 578 us -> 341 us (0.59)
  waiting for transfers between devices: 454 us -> 199 us
  starting transfers between devices: 36.9 us -> 77.7 us
  Pallas kernels: 0 us -> 32.1 us
  matrix products: 26 us -> 0 us
  between operations: 15.4 us -> 1.66 us
  other arithmetic: 17.3 us -> 8.99 us
    ppermute x2 -> x25, waiting for transfers between devices: 0.01 us -> 199 us  [move(): return lax.ppermute(array, ('section', 'peer'), pairs)]
    all_gather x2 -> x0, waiting for transfers between devices: 145 us -> none  [the longest x1 84.4 us: per_device(): lax.all_gather(in_weights, 'peer', axis=2, tiled=True)]
    all_to_all x2, waiting for transfers between devices: 112 us -> 0.01 us  [exchange(): lax.all_to_all(routed, 'peer', split_axis=0, concat_axis=0, tiled=True)]
    reduce_scatter x1 -> x0, waiting for transfers between devices: 103 us -> none  [per_device(): lax.psum_scatter(grad_in_part.astype(jnp.bfloat16), 'peer', scatter_dimen...]
    unnamed x5 -> x0, waiting for transfers between devices: 93.3 us -> none
    ppermute x2 -> x25, starting transfers between devices: 14.5 us -> 66.1 us  [move(): return lax.ppermute(array, ('section', 'peer'), pairs)]
    pallas_call x0 -> x3, Pallas kernels: none -> 32.1 us  [the longest x1 15.8 us: per_device(): pl.pallas_call(functools.partial(back_kernel, spans, share), out_shape=[f...]
    dot_general x17 -> x0, matrix products: 26 us -> none  [the longest x4 8.65 us: contract_cols(): lax.dot_general(left, right, (((1,), (1,)), ((), ())), preferred_element_...]
  transfers between devices with their start and end apart: 8 -> 27, of which waited for: 6 -> 11; matrix products, arithmetic and copies ran while one was open for 7% -> 5% of each run, Pallas kernels for 0% -> 5%
where the time goes in v1:
time: 341 us
  waiting for transfers between devices  199 us (58%)
  starting transfers between devices  77.7 us (23%)
  Pallas kernels  32.1 us (9%)
  local copies, waits for them, and re-layouts  21 us (6%)
  other arithmetic  8.99 us (3%)
    ppermute x25, waiting for transfers between devices, move(): return lax.ppermute(array, ('section', 'peer'), pairs)  199 us
    ppermute x25, starting transfers between devices, move(): return lax.ppermute(array, ('section', 'peer'), pairs)  66.1 us
    pallas_call x1, Pallas kernels, per_device(): pl.pallas_call(functools.partial(back_kernel, spans, share), out_shape=[f...  15.8 us
    pallas_call x1, Pallas kernels, per_device(): pl.pallas_call(functools.partial(forward_kernel, spans, share, slots), ou...  13.9 us
    all_to_all x2, starting transfers between devices, exchange(): lax.all_to_all(routed, 'peer', split_axis=0, concat_axis=0, tiled=True)  11.7 us
    unnamed x43, local copies, waits for them, and re-layouts  9.84 us
  transfers between devices with their start and end apart: 27, of which 11 were waited for; matrix products, arithmetic and copies ran while one was open for 5% of the time, Pallas kernels for 5%

profile of v1, /device:TPU:25, one launch (start us, length us, event | category | flops | bytes accessed | tf_op | source)
XLA Modules:
  0.0 340.8 jit_solution(9888851527963653324)
XLA Ops:
  0.7 1.1 constant_dynamic-update-slice_fusion.4
  1.7 0.9 constant_dynamic-update-slice_fusion.3
  2.7 3.1 collective-permute-start
  5.8 2.8 collective-permute-start.5
  8.6 0.9 collective-permute-start.4
  9.5 0.6 collective-permute-start.3
  10.1 3.1 collective-permute-start.1
  13.2 4.4 %collective-permute-start.2 = (bf16[464,384]{1,0:T(8,128)(2,1)S(1)}, bf16[464,384]{1,0:T(8,128)(2,1)S(1)}, u32[]{:S(2)}, u32[]{:S(2)}) collective-permute-start(bf16[464,384]{1,0:T(8,128)(2,1)S(1)} %pad_maximum_fusion.3), channel_id=1, source_target_pairs={{0,8},{1,9},{2,10},{3,11},{4,12},{5,13},{6,14},{7,15},{8,0},{9,1},... | collective-permute-start | bytes 1069064 | tf_op jit(solution)/shard_map/ppermute | solution.py:26
  17.7 1.8 collective-permute-done
  19.5 19.7 %collective-permute-done.1 = bf16[464,384]{1,0:T(8,128)(2,1)S(1)} collective-permute-done((bf16[464,384]{1,0:T(8,128)(2,1)S(1)}, bf16[464,384]{1,0:T(8,128)(2,1)S(1)}, u32[]{:S(2)}, u32[]{:S(2)}) %collective-permute-start.1) | collective-permute-done | bytes 356384 | tf_op jit(solution)/shard_map/ppermute | solution.py:26
  39.4 2.1 collective-permute-start.7
  41.6 5.5 %collective-permute-start.11 = (bf16[704,384]{1,0:T(8,128)(2,1)S(1)}, bf16[704,384]{1,0:T(8,128)(2,1)}, u32[]{:S(2)}, u32[]{:S(2)}) collective-permute-start(bf16[704,384]{1,0:T(8,128)(2,1)S(1)} %pad_maximum_fusion.refs_5_), channel_id=1, source_target_pairs={{0,12},{1,13},{2,14},{3,15},{4,0},{5,1},{6,2},{7,3},{8,4},{9,5},{1... | collective-permute-start | bytes 1622024 | tf_op jit(solution)/shard_map/ppermute | solution.py:26
  47.1 24.2 %collective-permute-done.7.refs_2_ = bf16[1856,384]{1,0:T(8,128)(2,1)S(1)} collective-permute-done((bf16[1856,384]{1,0:T(8,128)(2,1)S(1)}, bf16[1856,384]{1,0:T(8,128)(2,1)S(1)}, u32[]{:S(2)}, u32[]{:S(2)}) %collective-permute-start.7) | collective-permute-done | bytes 1425440 | tf_op jit(solution)/shard_map/ppermute | solution.py:26
  71.3 1.0 slice.113
  72.3 3.3 collective-permute-start.9
  75.6 1.1 slice.112
  76.6 0.6 dynamic_slice.3
  77.9 1.7 slice.115
  79.6 5.5 %collective-permute-start.13 = (bf16[352,384]{1,0:T(8,128)(2,1)}, bf16[352,384]{1,0:T(8,128)(2,1)}, u32[]{:S(2)}, u32[]{:S(2)}) collective-permute-start(bf16[352,384]{1,0:T(8,128)(2,1)} %slice.115), channel_id=1, source_target_pairs={{0,12},{1,13},{2,14},{3,15},{4,0},{5,1},{6,2},{7,3},{8,4},{9,5},{1... | collective-permute-start | bytes 811016 | tf_op jit(solution)/shard_map/ppermute | solution.py:26
  85.0 1.7 slice.114
  86.8 0.1 and.38
  87.1 2.8 collective-permute-done.13.refs_9_
  89.9 11.9 %collective-permute-done.12.refs_8_ = bf16[352,384]{1,0:T(8,128)(2,1)} collective-permute-done((bf16[352,384]{1,0:T(8,128)(2,1)}, bf16[352,384]{1,0:T(8,128)(2,1)}, u32[]{:S(2)}, u32[]{:S(2)}) %collective-permute-start.12) | collective-permute-done | bytes 270368 | tf_op jit(solution)/shard_map/ppermute | solution.py:26
  101.9 1.3 copy-done.3
  103.2 1.3 copy-done.4
  104.5 13.9 %shard_map.129 = bf16[16,16,5120]{2,1,0:T(8,128)(2,1)} custom-call(s32[2]{0:T(128)S(1)} %pad_add_fusion.where_ref, s32[16]{0:T(128)S(1)} %select_reduce_fusion.1.index_ref, f32[2,5120]{1,0:T(2,128)S(1)} %bitcast.100, bf16[128,5120]{1,0:T(8,128)(2,1)S(1)} %bitcast.99, bf16[1856,384]{1,0:T(8,128)(2,1)S(1)} %copy-done.3, ...), custom_call_target="tpu_custom_call" | custom-call | flops 12000000000 | bytes 36000000 | tf_op jit(solution)/shard_map/pallas_call | solution.py:400
  118.4 4.6 %all-to-all-start = ((bf16[16,16,5120]{2,1,0:T(8,128)(2,1)}), bf16[16,16,5120]{2,1,0:T(8,128)(2,1)}, u32[]{:S(2)}, u32[]{:S(2)}) async-start(bf16[16,16,5120]{2,1,0:T(8,128)(2,1)} %shard_map.129), calls=%async_computation | async-start | bytes 5242880 | tf_op jit(solution)/shard_map/all_to_all | solution.py:302
  123.1 1.3 bitcast_select_fusion.cot_ref
  124.3 15.8 %shard_map.130 = (bf16[128,5120]{1,0:T(8,128)(2,1)}, bf16[2,4,320,384]{3,2,1,0:T(8,128)(2,1)}, bf16[2,2,4,160,384]{4,3,2,1,0:T(8,128)(2,1)}, bf16[2,2,4,160,384]...) custom-call(s32[2]{0:T(128)S(1)} %pad_add_fusion.where_ref, ...), custom_call_target="tpu_custom_call" | custom-call | flops 24999999488 | bytes 75000000 | tf_op jit(solution)/shard_map/pallas_call | solution.py:415
  140.2 1.9 copy.16
  142.2 0.2 copy-done.7
  142.3 0.2 copy.17
  142.6 2.6 collective-permute-start.17
  145.2 7.9 %collective-permute-start.15 = (bf16[128,5120]{1,0:T(8,128)(2,1)S(1)}, bf16[128,5120]{1,0:T(8,128)(2,1)S(1)}, u32[]{:S(2)}, u32[]{:S(2)}) collective-permute-start(bf16[128,5120]{1,0:T(8,128)(2,1)S(1)} %copy-done.15), channel_id=1, source_target_pairs={{16,0},{17,1},{18,2},{19,3},{20,4},{21,5},{22,6},{23,7},{24,8},{25... | collective-permute-start | bytes 3932168 | tf_op jit(solution)/shard_map/ppermute | solution.py:26
  153.1 0.1 select_reduce_fusion
  153.2 1.9 collective-permute-start.14
  155.1 37.9 %collective-permute-done.14.index_ref = s32[16]{0:T(128)S(1)} collective-permute-done((s32[16]{0:T(128)S(1)}, s32[16]{0:T(128)S(1)}, u32[]{:S(2)}, u32[]{:S(2)}) %collective-permute-start.14) | collective-permute-done | bytes 96 | tf_op jit(solution)/shard_map/ppermute | solution.py:26
  193.0 2.4 shard_map.131
  195.4 8.8 %collective-permute-done.17 = bf16[2,2,4,160,384]{4,3,1,2,0:T(8,128)(2,1)S(1)} collective-permute-done((bf16[2,2,4,160,384]{4,3,1,2,0:T(8,128)(2,1)S(1)}, bf16[2,2,4,160,384]{4,3,1,2,0:T(8,128)(2,1)S(1)}, u32[]{:S(2)}, u32[]{:S(2)}) %collective-permute-start.17) | collective-permute-done | bytes 1966112 | tf_op jit(solution)/shard_map/ppermute | solution.py:26
  204.2 1.4 copy-done.8
  205.6 7.1 %all-to-all-start.1 = ((bf16[16,16,5120]{2,1,0:T(8,128)(2,1)}), bf16[16,16,5120]{2,1,0:T(8,128)(2,1)S(1)}, u32[]{:S(2)}, u32[]{:S(2)}) async-start(bf16[16,16,5120]{2,1,0:T(8,128)(2,1)} %shard_map.131), calls=%async_computation.1 | async-start | bytes 5242880 | tf_op jit(solution)/shard_map/all_to_all | solution.py:302
  212.7 1.9 fusion.1
  214.6 0.2 copy-done.9
  214.8 0.2 copy-done.13
  215.0 0.3 fusion.3
  215.3 1.7 collective-permute-start.18
  217.0 1.3 collective-permute-start.19
  218.3 29.5 %collective-permute-done.18 = bf16[2,4,160,384]{3,2,0,1:T(8,128)(2,1)S(1)} collective-permute-done((bf16[2,4,160,384]{3,2,0,1:T(8,128)(2,1)S(1)}, bf16[2,4,160,384]{3,2,0,1:T(8,128)(2,1)S(1)}, u32[]{:S(2)}, u32[]{:S(2)}) %collective-permute-start.18) | collective-permute-done | bytes 983072 | tf_op jit(solution)/shard_map/ppermute | solution.py:26
  247.7 0.4 fusion
  248.1 12.0 %collective-permute-start.24 = (bf16[16,16,5120]{2,1,0:T(8,128)(2,1)}, bf16[16,16,5120]{2,1,0:T(8,128)(2,1)}, u32[]{:S(2)}, u32[]{:S(2)}) collective-permute-start(bf16[16,16,5120]{2,1,0:T(8,128)(2,1)} %all-to-all-done), channel_id=1, source_target_pairs={{0,16},{1,17},{2,18},{3,19},{4,20},{5,21},{6,22},{7,23},{8,24},{9,... | collective-permute-start | bytes 7864328 | tf_op jit(solution)/shard_map/ppermute | solution.py:26
  260.2 1.6 fusion.2
  261.9 2.2 collective-permute-start.20
  264.1 1.6 collective-permute-start.21
  265.7 58.8 %collective-permute-done.20 = bf16[2,2,160,384]{3,2,1,0:T(8,128)(2,1)S(1)} collective-permute-done((bf16[2,2,160,384]{3,2,1,0:T(8,128)(2,1)S(1)}, bf16[2,2,160,384]{3,2,1,0:T(8,128)(2,1)S(1)}, u32[]{:S(2)}, u32[]{:S(2)}) %collective-permute-start.20) | collective-permute-done | bytes 491552 | tf_op jit(solution)/shard_map/ppermute | solution.py:26
  324.6 1.7 collective-permute-start.22
  326.3 2.0 collective-permute-start.23
  328.3 3.6 %collective-permute-done.22 = bf16[2,160,384]{2,1,0:T(8,128)(2,1)S(1)} collective-permute-done((bf16[2,160,384]{2,1,0:T(8,128)(2,1)S(1)}, bf16[2,160,384]{2,1,0:T(8,128)(2,1)S(1)}, u32[]{:S(2)}, u32[]{:S(2)}) %collective-permute-start.22) | collective-permute-done | bytes 245792 | tf_op jit(solution)/shard_map/ppermute | solution.py:26
  332.0 0.3 collective-permute-done.23
  332.3 0.9 convert_add_fusion.2
  333.2 1.1 constant_dynamic-update-slice_fusion.5
  334.2 0.7 slice_bitcast_fusion.1
  335.0 0.9 slice_bitcast_fusion
  335.9 3.5 %copy.42 = bf16[1,1,16,16,5120]{4,3,2,1,0:T(8,128)(2,1)} copy(bf16[1,1,16,16,5120]{4,3,2,1,0:T(8,128)(2,1)} %bitcast.32) | data formatting | bytes 5242880
  339.3 1.5 copy.43
  (70 shorter events, 1.1 us)
Async XLA Ops:
  0.6 5.1 %copy-start.11 = (bf16[1,2,128,320]{2,3,1,0:T(8,128)(2,1)S(1)}, bf16[1,2,128,320]{2,3,1,0:T(8,128)(2,1)}, u32[]{:S(2)}) copy-start(bf16[1,2,128,320]{2,3,1,0:T(8,128)(2,1)} %param.19) | copy-start | bytes 491524
  0.6 5.1 %copy-start.6 = (bf16[1,2,320,256]{3,2,1,0:T(8,128)(2,1)S(1)}, bf16[1,2,320,256]{3,2,1,0:T(8,128)(2,1)}, u32[]{:S(2)}) copy-start(bf16[1,2,320,256]{3,2,1,0:T(8,128)(2,1)} %param.18) | copy-start | bytes 983044
  2.7 16.8 %collective-permute-start = (bf16[464,384]{1,0:T(8,128)(2,1)S(1)}, bf16[464,384]{1,0:T(8,128)(2,1)S(1)}, u32[]{:S(2)}, u32[]{:S(2)}) collective-permute-start(bf16[464,384]{1,0:T(8,128)(2,1)S(1)} %pad_maximum_fusion.3), channel_id=1, source_target_pairs={{0,4},{1,5},{2,6},{3,7},{4,8},{5,9},{6,10},{7,11},{8,12},{9,13},{1... | collective-permute-start | bytes 1069064 | tf_op jit(solution)/shard_map/ppermute | solution.py:26
  5.8 7.4 %collective-permute-start.5 = (bf16[176,384]{1,0:T(8,128)(2,1)S(1)}, bf16[176,384]{1,0:T(8,128)(2,1)S(1)}, u32[]{:S(2)}, u32[]{:S(2)}) collective-permute-start(bf16[176,384]{1,0:T(8,128)(2,1)S(1)} %fusion.8), channel_id=1, source_target_pairs={{0,2},{1,3},{2,0},{3,1},{4,6},{5,7},{6,4},{7,5},{8,10},{9,11},{10,... | collective-permute-start | bytes 405512 | tf_op jit(solution)/shard_map/ppermute | solution.py:26
  8.6 9.0 %collective-permute-start.4 = (bf16[176,384]{1,0:T(8,128)(2,1)S(1)}, bf16[176,384]{1,0:T(8,128)(2,1)S(1)}, u32[]{:S(2)}, u32[]{:S(2)}) collective-permute-start(bf16[176,384]{1,0:T(8,128)(2,1)S(1)} %fusion.8), channel_id=1, source_target_pairs={{0,3},{1,0},{2,1},{3,2},{4,7},{5,4},{6,5},{7,6},{8,11},{9,8},{10,9... | collective-permute-start | bytes 405512 | tf_op jit(solution)/shard_map/ppermute | solution.py:26
  9.5 8.1 %collective-permute-start.3 = (bf16[176,384]{1,0:T(8,128)(2,1)S(1)}, bf16[176,384]{1,0:T(8,128)(2,1)S(1)}, u32[]{:S(2)}, u32[]{:S(2)}) collective-permute-start(bf16[176,384]{1,0:T(8,128)(2,1)S(1)} %fusion.8), channel_id=1, source_target_pairs={{0,1},{1,2},{2,3},{3,0},{4,5},{5,6},{6,7},{7,4},{8,9},{9,10},{10,1... | collective-permute-start | bytes 405512 | tf_op jit(solution)/shard_map/ppermute | solution.py:26
  10.1 29.1 %collective-permute-start.1 = (bf16[464,384]{1,0:T(8,128)(2,1)S(1)}, bf16[464,384]{1,0:T(8,128)(2,1)S(1)}, u32[]{:S(2)}, u32[]{:S(2)}) collective-permute-start(bf16[464,384]{1,0:T(8,128)(2,1)S(1)} %pad_maximum_fusion.3), channel_id=1, source_target_pairs={{0,12},{1,13},{2,14},{3,15},{4,0},{5,1},{6,2},{7,3},{8,4},{9,5},{1... | collective-permute-start | bytes 1069064 | tf_op jit(solution)/shard_map/ppermute | solution.py:26
  13.2 26.1 %collective-permute-start.2 = (bf16[464,384]{1,0:T(8,128)(2,1)S(1)}, bf16[464,384]{1,0:T(8,128)(2,1)S(1)}, u32[]{:S(2)}, u32[]{:S(2)}) collective-permute-start(bf16[464,384]{1,0:T(8,128)(2,1)S(1)} %pad_maximum_fusion.3), channel_id=1, source_target_pairs={{0,8},{1,9},{2,10},{3,11},{4,12},{5,13},{6,14},{7,15},{8,0},{9,1},... | collective-permute-start | bytes 1069064 | tf_op jit(solution)/shard_map/ppermute | solution.py:26
  39.3 37.4 %copy-start.16 = (s32[16]{0:T(128)S(1)}, s32[16]{0:T(128)}, u32[]{:S(2)}) copy-start(s32[16]{0:T(128)} %param.14) | copy-start | bytes 196
  39.4 36.2 %copy-start.2 = (bf16[1856,384]{1,0:T(8,128)(2,1)}, bf16[1856,384]{1,0:T(8,128)(2,1)S(1)}, u32[]{:S(2)}) copy-start(bf16[1856,384]{1,0:T(8,128)(2,1)S(1)} %constant_dynamic-update-slice_fusion.refs_0_) | copy-start | bytes 4276228
  39.4 47.4 %copy-start.14 = (s32[1,1,8]{2,1,0:T(1,128)S(1)}, s32[1,1,8]{2,1,0:T(1,128)}, u32[]{:S(2)}) copy-start(s32[1,1,8]{2,1,0:T(1,128)} %param.13) | copy-start | bytes 100
  39.4 47.6 %copy-start.17 = (s32[1,1,8]{2,1,0:T(1,128)S(1)}, s32[1,1,8]{2,1,0:T(1,128)}, u32[]{:S(2)}) copy-start(s32[1,1,8]{2,1,0:T(1,128)} %param.15) | copy-start | bytes 100
  39.4 62.5 %copy-start.5 = (f32[1,2,5120]{2,1,0:T(2,128)S(1)}, f32[1,2,5120]{2,1,0:T(2,128)}, u32[]{:S(2)}) copy-start(f32[1,2,5120]{2,1,0:T(2,128)} %param.17) | copy-start | bytes 122884
  39.4 31.9 %collective-permute-start.7 = (bf16[1856,384]{1,0:T(8,128)(2,1)S(1)}, bf16[1856,384]{1,0:T(8,128)(2,1)S(1)}, u32[]{:S(2)}, u32[]{:S(2)}) collective-permute-start(bf16[1856,384]{1,0:T(8,128)(2,1)S(1)} %constant_dynamic-update-slice_fusion.refs_0_), channel_id=1, source_target_pairs={{0,3},{1,0},{2,1},{3,2},{4,7},{5,4},{6,5},{7,6},{8,11},{9,8},{10,9... | collective-permute-start | bytes 4276232 | tf_op jit(solution)/shard_map/ppermute | solution.py:26
  41.6 34.0 %collective-permute-start.6 = (bf16[1856,384]{1,0:T(8,128)(2,1)S(1)}, bf16[1856,384]{1,0:T(8,128)(2,1)S(1)}, u32[]{:S(2)}, u32[]{:S(2)}) collective-permute-start(bf16[1856,384]{1,0:T(8,128)(2,1)S(1)} %constant_dynamic-update-slice_fusion.refs_0_), channel_id=1, source_target_pairs={{0,1},{1,2},{2,3},{3,0},{4,5},{5,6},{6,7},{7,4},{8,9},{9,10},{10,1... | collective-permute-start | bytes 4276232 | tf_op jit(solution)/shard_map/ppermute | solution.py:26
  41.6 36.3 %collective-permute-start.11 = (bf16[704,384]{1,0:T(8,128)(2,1)S(1)}, bf16[704,384]{1,0:T(8,128)(2,1)}, u32[]{:S(2)}, u32[]{:S(2)}) collective-permute-start(bf16[704,384]{1,0:T(8,128)(2,1)S(1)} %pad_maximum_fusion.refs_5_), channel_id=1, source_target_pairs={{0,12},{1,13},{2,14},{3,15},{4,0},{5,1},{6,2},{7,3},{8,4},{9,5},{1... | collective-permute-start | bytes 1622024 | tf_op jit(solution)/shard_map/ppermute | solution.py:26
  47.1 38.0 %collective-permute-start.10 = (bf16[704,384]{1,0:T(8,128)(2,1)S(1)}, bf16[704,384]{1,0:T(8,128)(2,1)}, u32[]{:S(2)}, u32[]{:S(2)}) collective-permute-start(bf16[704,384]{1,0:T(8,128)(2,1)S(1)} %pad_maximum_fusion.refs_5_), channel_id=1, source_target_pairs={{0,4},{1,5},{2,6},{3,7},{4,8},{5,9},{6,10},{7,11},{8,12},{9,13},{1... | collective-permute-start | bytes 1622024 | tf_op jit(solution)/shard_map/ppermute | solution.py:26
  71.3 30.6 %copy-start = (bf16[1856,384]{1,0:T(8,128)(2,1)}, bf16[1856,384]{1,0:T(8,128)(2,1)S(1)}, u32[]{:S(2)}) copy-start(bf16[1856,384]{1,0:T(8,128)(2,1)S(1)} %collective-permute-done.7.refs_2_) | copy-start | bytes 4276228
  72.3 29.6 %collective-permute-start.9 = (bf16[928,384]{1,0:T(8,128)(2,1)}, bf16[928,384]{1,0:T(8,128)(2,1)}, u32[]{:S(2)}, u32[]{:S(2)}) collective-permute-start(bf16[928,384]{1,0:T(8,128)(2,1)} %slice.113), channel_id=1, source_target_pairs={{0,3},{1,0},{2,1},{3,2},{4,7},{5,4},{6,5},{7,6},{8,11},{9,8},{10,9... | collective-permute-start | bytes 2138120 | tf_op jit(solution)/shard_map/ppermute | solution.py:26
  75.6 42.8 %copy-start.1 = (bf16[1856,384]{1,0:T(8,128)(2,1)}, bf16[1856,384]{1,0:T(8,128)(2,1)S(1)}, u32[]{:S(2)}) copy-start(bf16[1856,384]{1,0:T(8,128)(2,1)S(1)} %collective-permute-done.6.refs_1_) | copy-start | bytes 4276228
  76.6 25.2 %collective-permute-start.8 = (bf16[928,384]{1,0:T(8,128)(2,1)}, bf16[928,384]{1,0:T(8,128)(2,1)}, u32[]{:S(2)}, u32[]{:S(2)}) collective-permute-start(bf16[928,384]{1,0:T(8,128)(2,1)} %slice.112), channel_id=1, source_target_pairs={{0,1},{1,2},{2,3},{3,0},{4,5},{5,6},{6,7},{7,4},{8,9},{9,10},{10,1... | collective-permute-start | bytes 2138120 | tf_op jit(solution)/shard_map/ppermute | solution.py:26
  79.6 10.3 %collective-permute-start.13 = (bf16[352,384]{1,0:T(8,128)(2,1)}, bf16[352,384]{1,0:T(8,128)(2,1)}, u32[]{:S(2)}, u32[]{:S(2)}) collective-permute-start(bf16[352,384]{1,0:T(8,128)(2,1)} %slice.115), channel_id=1, source_target_pairs={{0,12},{1,13},{2,14},{3,15},{4,0},{5,1},{6,2},{7,3},{8,4},{9,5},{1... | collective-permute-start | bytes 811016 | tf_op jit(solution)/shard_map/ppermute | solution.py:26
  86.7 15.1 %collective-permute-start.12 = (bf16[352,384]{1,0:T(8,128)(2,1)}, bf16[352,384]{1,0:T(8,128)(2,1)}, u32[]{:S(2)}, u32[]{:S(2)}) collective-permute-start(bf16[352,384]{1,0:T(8,128)(2,1)} %slice.114), channel_id=1, source_target_pairs={{0,4},{1,5},{2,6},{3,7},{4,8},{5,9},{6,10},{7,11},{8,12},{9,13},{1... | collective-permute-start | bytes 811016 | tf_op jit(solution)/shard_map/ppermute | solution.py:26
  101.9 1.4 copy-start.3
  103.2 1.3 copy-start.4
  118.4 4.6 %copy-start.12 = (bf16[1,1,8,16,5120]{4,3,2,1,0:T(8,128)(2,1)S(1)}, bf16[1,1,8,16,5120]{4,3,2,1,0:T(8,128)(2,1)}, u32[]{:S(2)}) copy-start(bf16[1,1,8,16,5120]{4,3,2,1,0:T(8,128)(2,1)} %param.12) | copy-start | bytes 3932164
  118.4 87.2 %all-to-all-start = ((bf16[16,16,5120]{2,1,0:T(8,128)(2,1)}), bf16[16,16,5120]{2,1,0:T(8,128)(2,1)}, u32[]{:S(2)}, u32[]{:S(2)}) async-start(bf16[16,16,5120]{2,1,0:T(8,128)(2,1)} %shard_map.129), calls=%async_computation | async-start | bytes 5242880 | tf_op jit(solution)/shard_map/all_to_all | solution.py:302
  140.2 2.1 copy-start.7
  142.3 2.9 copy-start.15
  142.3 10.8 %copy-start.18 = (s32[1,1,8]{2,1,0:T(1,128)S(1)}, s32[1,1,8]{2,1,0:T(1,128)}, u32[]{:S(2)}) copy-start(s32[1,1,8]{2,1,0:T(1,128)} %param.16) | copy-start | bytes 100
  142.6 61.6 %collective-permute-start.17 = (bf16[2,2,4,160,384]{4,3,1,2,0:T(8,128)(2,1)S(1)}, bf16[2,2,4,160,384]{4,3,1,2,0:T(8,128)(2,1)S(1)}, u32[]{:S(2)}, u32[]{:S(2)}) collective-permute-start(bf16[2,2,4,160,384]{4,3,1,2,0:T(8,128)(2,1)S(1)} %copy.17), channel_id=1, source_target_pairs={{0,3},{1,0},{2,1},{3,2},{4,7},{5,4},{6,5},{7,6},{8,11},{9,8},{10,9... | collective-permute-start | bytes 5898248 | tf_op jit(solution)/shard_map/ppermute | solution.py:26
  145.2 60.4 %collective-permute-start.16 = (bf16[2,2,4,160,384]{4,3,1,2,0:T(8,128)(2,1)S(1)}, bf16[2,2,4,160,384]{4,3,1,2,0:T(8,128)(2,1)}, u32[]{:S(2)}, u32[]{:S(2)}) collective-permute-start(bf16[2,2,4,160,384]{4,3,1,2,0:T(8,128)(2,1)S(1)} %copy.16), channel_id=1, source_target_pairs={{0,1},{1,2},{2,3},{3,0},{4,5},{5,6},{6,7},{7,4},{8,9},{9,10},{10,1... | collective-permute-start | bytes 5898248 | tf_op jit(solution)/shard_map/ppermute | solution.py:26
  145.2 47.8 %collective-permute-start.15 = (bf16[128,5120]{1,0:T(8,128)(2,1)S(1)}, bf16[128,5120]{1,0:T(8,128)(2,1)S(1)}, u32[]{:S(2)}, u32[]{:S(2)}) collective-permute-start(bf16[128,5120]{1,0:T(8,128)(2,1)S(1)} %copy-done.15), channel_id=1, source_target_pairs={{16,0},{17,1},{18,2},{19,3},{20,4},{21,5},{22,6},{23,7},{24,8},{25... | collective-permute-start | bytes 3932168 | tf_op jit(solution)/shard_map/ppermute | solution.py:26
  153.2 39.8 %collective-permute-start.14 = (s32[16]{0:T(128)S(1)}, s32[16]{0:T(128)S(1)}, u32[]{:S(2)}, u32[]{:S(2)}) collective-permute-start(s32[16]{0:T(128)S(1)} %select_reduce_fusion), channel_id=1, source_target_pairs={{16,0},{17,1},{18,2},{19,3},{20,4},{21,5},{22,6},{23,7},{24,8},{25... | collective-permute-start | bytes 200 | tf_op jit(solution)/shard_map/ppermute | solution.py:26
  204.2 1.4 copy-start.8
  205.6 127.5 %all-to-all-start.1 = ((bf16[16,16,5120]{2,1,0:T(8,128)(2,1)}), bf16[16,16,5120]{2,1,0:T(8,128)(2,1)S(1)}, u32[]{:S(2)}, u32[]{:S(2)}) async-start(bf16[16,16,5120]{2,1,0:T(8,128)(2,1)} %shard_map.131), calls=%async_computation.1 | async-start | bytes 5242880 | tf_op jit(solution)/shard_map/all_to_all | solution.py:302
  212.7 2.1 copy-start.9
  212.7 2.4 copy-start.13
  214.6 33.2 %copy-start.10 = (bf16[2,4,320,384]{3,2,1,0:T(8,128)(2,1)S(1)}, bf16[2,4,320,384]{3,2,1,0:T(8,128)(2,1)}, u32[]{:S(2)}) copy-start(bf16[2,4,320,384]{3,2,1,0:T(8,128)(2,1)} %get-tuple-element.27) | copy-start | bytes 5898244
  215.3 32.4 %collective-permute-start.18 = (bf16[2,4,160,384]{3,2,0,1:T(8,128)(2,1)S(1)}, bf16[2,4,160,384]{3,2,0,1:T(8,128)(2,1)S(1)}, u32[]{:S(2)}, u32[]{:S(2)}) collective-permute-start(bf16[2,4,160,384]{3,2,0,1:T(8,128)(2,1)S(1)} %fusion.1), channel_id=1, source_target_pairs={{0,1},{1,2},{2,3},{3,0},{4,5},{5,6},{6,7},{7,4},{8,9},{9,10},{10,1... | collective-permute-start | bytes 2949128 | tf_op jit(solution)/shard_map/ppermute | solution.py:26
  217.0 43.2 %collective-permute-start.19 = (bf16[2,4,160,384]{3,2,1,0:T(8,128)(2,1)S(1)}, bf16[2,4,160,384]{3,2,1,0:T(8,128)(2,1)S(1)}, u32[]{:S(2)}, u32[]{:S(2)}) collective-permute-start(bf16[2,4,160,384]{3,2,1,0:T(8,128)(2,1)S(1)} %fusion.3), channel_id=1, source_target_pairs={{0,3},{1,0},{2,1},{3,2},{4,7},{5,4},{6,5},{7,6},{8,11},{9,8},{10,9... | collective-permute-start | bytes 2949128 | tf_op jit(solution)/shard_map/ppermute | solution.py:26
  248.1 85.0 %collective-permute-start.24 = (bf16[16,16,5120]{2,1,0:T(8,128)(2,1)}, bf16[16,16,5120]{2,1,0:T(8,128)(2,1)}, u32[]{:S(2)}, u32[]{:S(2)}) collective-permute-start(bf16[16,16,5120]{2,1,0:T(8,128)(2,1)} %all-to-all-done), channel_id=1, source_target_pairs={{0,16},{1,17},{2,18},{3,19},{4,20},{5,21},{6,22},{7,23},{8,24},{9,... | collective-permute-start | bytes 7864328 | tf_op jit(solution)/shard_map/ppermute | solution.py:26
  261.9 62.6 %collective-permute-start.20 = (bf16[2,2,160,384]{3,2,1,0:T(8,128)(2,1)S(1)}, bf16[2,2,160,384]{3,2,1,0:T(8,128)(2,1)S(1)}, u32[]{:S(2)}, u32[]{:S(2)}) collective-permute-start(bf16[2,2,160,384]{3,2,1,0:T(8,128)(2,1)S(1)} %pad_maximum_fusion.1), channel_id=1, source_target_pairs={{0,4},{1,5},{2,6},{3,7},{4,8},{5,9},{6,10},{7,11},{8,12},{9,13},{1... | collective-permute-start | bytes 1474568 | tf_op jit(solution)/shard_map/ppermute | solution.py:26
  264.1 60.4 %collective-permute-start.21 = (bf16[2,2,160,384]{3,2,1,0:T(8,128)(2,1)S(1)}, bf16[2,2,160,384]{3,2,1,0:T(8,128)(2,1)S(1)}, u32[]{:S(2)}, u32[]{:S(2)}) collective-permute-start(bf16[2,2,160,384]{3,2,1,0:T(8,128)(2,1)S(1)} %pad_maximum_fusion.2), channel_id=1, source_target_pairs={{0,12},{1,13},{2,14},{3,15},{4,0},{5,1},{6,2},{7,3},{8,4},{9,5},{1... | collective-permute-start | bytes 1474568 | tf_op jit(solution)/shard_map/ppermute | solution.py:26
  324.6 7.2 %collective-permute-start.22 = (bf16[2,160,384]{2,1,0:T(8,128)(2,1)S(1)}, bf16[2,160,384]{2,1,0:T(8,128)(2,1)S(1)}, u32[]{:S(2)}, u32[]{:S(2)}) collective-permute-start(bf16[2,160,384]{2,1,0:T(8,128)(2,1)S(1)} %fusion.5), channel_id=1, source_target_pairs={{0,4},{1,5},{2,6},{3,7},{4,8},{5,9},{6,10},{7,11},{8,12},{9,13},{1... | collective-permute-start | bytes 737288 | tf_op jit(solution)/shard_map/ppermute | solution.py:26
  326.3 5.9 %collective-permute-start.23 = (bf16[2,160,384]{2,1,0:T(8,128)(2,1)S(1)}, bf16[2,160,384]{2,1,0:T(8,128)(2,1)S(1)}, u32[]{:S(2)}, u32[]{:S(2)}) collective-permute-start(bf16[2,160,384]{2,1,0:T(8,128)(2,1)S(1)} %fusion.4), channel_id=1, source_target_pairs={{0,12},{1,13},{2,14},{3,15},{4,0},{5,1},{6,2},{7,3},{8,4},{9,5},{1... | collective-permute-start | bytes 737288 | tf_op jit(solution)/shard_map/ppermute | solution.py:26

commit v2 on v1

--- a/solution.py
+++ b/solution.py
@@ -159,9 +159,9 @@
             routed_ref[peer] = jnp.zeros((slots, rows_ref.shape[1]), rows_ref.dtype)
 
 
-def forward_kernel(spans, share, slots, where_ref, index_ref, gain_ref, input_ref, *refs):
+def forward_kernel(spans, share, where_ref, gain_ref, input_ref, *refs):
     blocks = refs[: len(spans)]
-    routed_ref, low_full_ref, high_full_ref, stream_ref, rows_ref, sems = refs[len(spans) :]
+    rows_ref, low_full_ref, high_full_ref, stream_ref, sems = refs[len(spans) :]
     copies = put_together((low_full_ref, high_full_ref), blocks, spans, where_ref, share, sems)
     rank = low_full_ref.shape[1] // 3
     steps = input_ref.shape[1] // CHUNK
@@ -187,7 +187,6 @@
         return carry
 
     loop(steps, upper, 0)
-    hand_out(index_ref, rows_ref, routed_ref, slots)
 
 
 def spread_kernel(slots, index_ref, rows_ref, routed_ref):
@@ -277,13 +276,13 @@
         for dz in range(ROW):
             z = lax.rem(where_ref[0] + dz, ROW) * ROW
             own, ahead, far, behind = (z + lax.rem(where_ref[1] + dx, ROW) for dx in range(ROW))
-            own_ref[layer, dz] = grad_ref[layer, own]
-            up_ref[0, layer, dz] = grad_ref[layer, far, :half]
-            up_ref[1, layer, dz] = grad_ref[layer, ahead, half:]
-            down_ref[0, layer, dz] = grad_ref[layer, far, half:]
-            down_ref[1, layer, dz] = grad_ref[layer, behind, :half]
-            next_ref[layer, dz] = grad_ref[layer, ahead, :half]
-            last_ref[layer, dz] = grad_ref[layer, behind, half:]
+            own_ref[dz, layer] = grad_ref[layer, own]
+            up_ref[0, dz, layer] = grad_ref[layer, far, :half]
+            up_ref[1, dz, layer] = grad_ref[layer, ahead, half:]
+            down_ref[0, dz, layer] = grad_ref[layer, far, half:]
+            down_ref[1, dz, layer] = grad_ref[layer, behind, :half]
+            next_ref[dz, layer] = grad_ref[layer, ahead, :half]
+            last_ref[dz, layer] = grad_ref[layer, behind, half:]
 
 
 def vmem(count):
@@ -300,6 +299,22 @@
 
 def exchange(routed):
     return lax.all_to_all(routed, "peer", split_axis=0, concat_axis=0, tiled=True)
+
+
+def settle_kernel(from_ref, to_ref):
+    to_ref[...] = from_ref[...]
+
+
+def settle(array):
+    step = pl.BlockSpec((2,) + array.shape[1:], lambda i: (i, 0, 0))
+    return pl.pallas_call(
+        settle_kernel,
+        out_shape=jax.ShapeDtypeStruct(array.shape, array.dtype),
+        grid=(array.shape[0] // 2,),
+        in_specs=[step],
+        out_specs=step,
+        cost_estimate=cost(3),
+    )(array)
 
 
 def slots_of(targets, active):
@@ -335,13 +350,10 @@
     dtype = own.dtype
     low, high = scatter_rest(own, ahead, behind, got_up, got_down, "x")
     low, high = low.astype(dtype), high.astype(dtype)
-    up, down = scatter_first(
-        jnp.stack([low[:, 2], high[:, 1]]), jnp.stack([high[:, 2], low[:, 3]]), "z"
-    )
-    mine = jnp.concatenate([low[:, 0], high[:, 0]], axis=1)
-    low, high = scatter_rest(mine, low[:, 1], high[:, 3], up, down, "z")
-    low, high, after = lax.optimization_barrier((low, high, after))
-    return jnp.concatenate([low, high], axis=1), after
+    up, down = scatter_first(jnp.stack([low[2], high[1]]), jnp.stack([high[2], low[3]]), "z")
+    up, down, after = lax.optimization_barrier((up, down, after))
+    mine = jnp.concatenate([low[0], high[0]], axis=1)
+    return jnp.concatenate(scatter_rest(mine, low[1], high[3], up, down, "z"), axis=1), after
 
 
 def cost(micros):
@@ -375,12 +387,12 @@
     cut = share * 45 // 100 // 16 * 16
     by_z = near_gather(jnp.concatenate([both[0], both[1, :cut]], axis=0), "z")
     by_x = near_gather(both[1, cut:], "x")
-    by_z, by_x = lax.optimization_barrier((by_z, by_x))
+    forward_slots = move(slots_of(wiring[0, 0], active), 0, 0, 1)
+    back_slots = move(slots_of(back_wiring[0, 0], active), 0, 0, -1)
+    by_z, by_x, forward_slots, back_slots = lax.optimization_barrier((by_z, by_x, forward_slots, back_slots))
     blocks = far_gather(by_z, "x", [(0, 0, share), (1, 0, cut)])
     blocks += far_gather(by_x, "z", [(1, cut, share - cut)])
 
-    forward_slots = slots_of(wiring[0, 0], active)
-    back_slots = move(slots_of(back_wiring[0, 0], active), 0, 0, -1)
     positions = jnp.arange(slots, dtype=jnp.int32)
     live = (positions[None, :] < lengths[0, 0][:, None]) & active
     cot = jnp.where(live[:, :, None], cotangents[0, 0], jnp.zeros((), cotangents.dtype))
@@ -397,24 +409,21 @@
     anywhere = [pl.BlockSpec(memory_space=pl.ANY)] * len(spans)
     wide = [pltpu.VMEM((width, 3 * rank), bf16)] * 2
     sems = pltpu.SemaphoreType.DMA((sum(len(held) for held in spans),))
-    outgoing = pl.pallas_call(
-        functools.partial(forward_kernel, spans, share, slots),
-        out_shape=routed,
-        in_specs=smem(2) + vmem(2) + anywhere,
-        out_specs=vmem(1)[0],
-        scratch_shapes=wide + [pltpu.VMEM((count, width), f32), pltpu.VMEM((count, width), bf16), sems],
-        compiler_params=pltpu.CompilerParams(vmem_limit_bytes=40 << 20),
-        cost_estimate=cost(12),
-    )(where, forward_slots, gains, forward_inputs.reshape(count, width), *arrays)
-
-    outgoing, saved = lax.optimization_barrier((outgoing, saved))
-    forward_arrived = move(exchange(outgoing), 0, 0, 1)
-
-    part = shaped(2, ROW, share // 2, 3 * rank)
-    pair = shaped(2, 2, ROW, share // 2, 3 * rank)
+    def spread(index, rows):
+        return pl.pallas_call(
+            functools.partial(spread_kernel, slots),
+            out_shape=routed,
+            in_specs=smem(1) + vmem(1),
+            out_specs=vmem(1)[0],
+            compiler_params=pltpu.CompilerParams(vmem_limit_bytes=16 << 20),
+            cost_estimate=cost(2),
+        )(index, rows)
+
+    part = shaped(ROW, 2, share // 2, 3 * rank)
+    pair = shaped(2, ROW, 2, share // 2, 3 * rank)
     d_rows, own, up, down, ahead, behind = pl.pallas_call(
         functools.partial(back_kernel, spans, share),
-        out_shape=[flat, shaped(2, ROW, share, 3 * rank), pair, pair, part, part],
+        out_shape=[flat, shaped(ROW, 2, share, 3 * rank), pair, pair, part, part],
         in_specs=smem(1) + vmem(3) + anywhere,
         out_specs=vmem(6),
         scratch_shapes=wide
@@ -429,18 +438,27 @@
         compiler_params=pltpu.CompilerParams(vmem_limit_bytes=52 << 20),
         cost_estimate=cost(25),
     )(where, gains, saved, cot, *arrays)
-    returned = pl.pallas_call(
-        functools.partial(spread_kernel, slots),
-        out_shape=routed,
-        in_specs=smem(1) + vmem(1),
+    d_rows, up, down, inputs = lax.optimization_barrier(
+        (d_rows, up, down, forward_inputs.reshape(count, width))
+    )
+    got_up, got_down = scatter_first(up, down, "x")
+    shifted = move(d_rows, 0, 0, -1)
+    rows = pl.pallas_call(
+        functools.partial(forward_kernel, spans, share),
+        out_shape=flat,
+        in_specs=smem(1) + vmem(2) + anywhere,
         out_specs=vmem(1)[0],
-        compiler_params=pltpu.CompilerParams(vmem_limit_bytes=16 << 20),
-        cost_estimate=cost(2),
-    )(back_slots, move(d_rows, 0, 0, -1))
-    got_up, got_down = scatter_first(up, down, "x")
-    returned, got_up, got_down = lax.optimization_barrier((returned, got_up, got_down))
-    backward_arrived = exchange(returned)
-    total, forward_arrived = reduce_scatter(own, ahead, behind, got_up, got_down, forward_arrived)
+        scratch_shapes=wide + [pltpu.VMEM((count, width), f32), sems],
+        compiler_params=pltpu.CompilerParams(vmem_limit_bytes=40 << 20),
+        cost_estimate=cost(12),
+    )(where, gains, inputs, *arrays)
+
+    shifted, rows = lax.optimization_barrier((shifted, rows))
+    backward_arrived = settle(exchange(spread(back_slots, shifted)))
+    outgoing = spread(forward_slots, move(rows, 0, 0, 1))
+    outgoing, got_up, got_down = lax.optimization_barrier((outgoing, got_up, got_down))
+    forward_arrived = exchange(outgoing)
+    total, backward_arrived = reduce_scatter(own, ahead, behind, got_up, got_down, backward_arrived)
 
     grad_in = total[:, :, : 2 * rank]
     grad_down = jnp.swapaxes(total[:, :, 2 * rank :], 1, 2)

time: 341 us -> 332 us (0.974)
  waiting for transfers between devices: 199 us -> 181 us
  local copies, waits for them, and re-layouts: 21 us -> 10.3 us
  other arithmetic: 8.99 us -> 17.8 us
  starting transfers between devices: 77.7 us -> 82.4 us
  Pallas kernels: 32.1 us -> 36.8 us
    ppermute x25 -> x26, waiting for transfers between devices: 199 us -> 181 us  [move(): return lax.ppermute(array, ('section', 'peer'), pairs)]
    unnamed x43 -> x35, local copies, waits for them, and re-layouts: 9.84 us -> 3.39 us
    pallas_call x2 -> x4, Pallas kernels: 16.3 us -> 20.8 us  [the longest x1 10.1 us: per_device(): pl.pallas_call(functools.partial(forward_kernel, spans, share), out_shape...]
    ppermute x25 -> x26, starting transfers between devices: 66.1 us -> 70.1 us  [move(): return lax.ppermute(array, ('section', 'peer'), pairs)]
    convert_element_type x2, other arithmetic: 0.33 us -> 3.86 us  [scatter_rest(): behind = add_up(behind, got_down[0]).astype(own.dtype)]
  transfers between devices with their start and end apart: 27 -> 28, of which waited for: 11 -> 14; matrix products, arithmetic and copies ran while one was open for 5% -> 7% of each run, Pallas kernels for 5% -> 6%
where the time goes in v2:
time: 332 us; the launch traced here: 330 us
  waiting for transfers between devices  181 us (55%)
  starting transfers between devices  82.4 us (25%)
  Pallas kernels  36.8 us (11%)
  other arithmetic  17.8 us (5%)
  local copies, waits for them, and re-layouts  10.3 us (3%)
    ppermute x26, waiting for transfers between devices, move(): return lax.ppermute(array, ('section', 'peer'), pairs)  181 us
    ppermute x26, starting transfers between devices, move(): return lax.ppermute(array, ('section', 'peer'), pairs)  70.1 us
    pallas_call x1, Pallas kernels, per_device(): pl.pallas_call(functools.partial(back_kernel, spans, share), out_shape=[f...  16.1 us
    all_to_all x2, starting transfers between devices, exchange(): lax.all_to_all(routed, 'peer', split_axis=0, concat_axis=0, tiled=True)  12.2 us
    pallas_call x1, Pallas kernels, per_device(): pl.pallas_call(functools.partial(forward_kernel, spans, share), out_shape...  10.1 us
  transfers between devices with their start and end apart: 28, of which 14 were waited for; matrix products, arithmetic and copies ran while one was open for 7% of the time, Pallas kernels for 6%

profile of v2, /device:TPU:25, one launch (start us, length us, event | category | flops | bytes accessed | tf_op | source)
XLA Modules:
  0.0 330.4 jit_solution(14537480817655819816)
XLA Ops:
  0.7 1.7 constant_dynamic-update-slice_fusion.4
  2.4 1.6 constant_dynamic-update-slice_fusion.3
  4.0 3.1 collective-permute-start
  7.1 2.8 collective-permute-start.5
  10.0 0.9 collective-permute-start.4
  10.8 0.6 collective-permute-start.3
  11.4 3.1 collective-permute-start.1
  14.5 0.6 dynamic_slice.3
  15.9 4.5 %collective-permute-start.2 = (bf16[464,384]{1,0:T(8,128)(2,1)S(1)}, bf16[464,384]{1,0:T(8,128)(2,1)S(1)}, u32[]{:S(2)}, u32[]{:S(2)}) collective-permute-start(bf16[464,384]{1,0:T(8,128)(2,1)S(1)} %pad_maximum_fusion.3), channel_id=1, source_target_pairs={{0,8},{1,9},{2,10},{3,11},{4,12},{5,13},{6,14},{7,15},{8,0},{9,1},... | collective-permute-start | bytes 1069064 | tf_op jit(solution)/shard_map/ppermute | solution.py:26
  20.5 4.5 %collective-permute-start.6 = (s32[16]{0:T(128)S(1)}, s32[16]{0:T(128)S(1)}, u32[]{:S(2)}, u32[]{:S(2)}) collective-permute-start(s32[16]{0:T(128)S(1)} %select_reduce_fusion.1), channel_id=1, source_target_pairs={{0,16},{1,17},{2,18},{3,19},{4,20},{5,21},{6,22},{7,23},{8,24},{9,... | collective-permute-start | bytes 200 | tf_op jit(solution)/shard_map/ppermute | solution.py:26
  25.0 1.9 collective-permute-start.7
  27.0 0.8 constant_dynamic-update-slice_fusion.2
  27.8 12.8 %collective-permute-done.1 = bf16[464,384]{1,0:T(8,128)(2,1)S(1)} collective-permute-done((bf16[464,384]{1,0:T(8,128)(2,1)S(1)}, bf16[464,384]{1,0:T(8,128)(2,1)S(1)}, u32[]{:S(2)}, u32[]{:S(2)}) %collective-permute-start.1) | collective-permute-done | bytes 356384 | tf_op jit(solution)/shard_map/ppermute | solution.py:26
  40.6 0.8 constant_dynamic-update-slice_fusion.1
  41.3 0.8 constant_dynamic-update-slice_fusion.refs_0_
  42.1 4.3 %collective-permute-done.7.index_ref = s32[16]{0:T(128)S(1)} collective-permute-done((s32[16]{0:T(128)S(1)}, s32[16]{0:T(128)S(1)}, u32[]{:S(2)}, u32[]{:S(2)}) %collective-permute-start.7) | collective-permute-done | bytes 96 | tf_op jit(solution)/shard_map/ppermute | solution.py:26
  46.4 2.1 collective-permute-start.9
  49.0 1.8 collective-permute-start.12
  51.0 9.3 %collective-permute-done.13.refs_7_ = bf16[704,384]{1,0:T(8,128)(2,1)} collective-permute-done((bf16[704,384]{1,0:T(8,128)(2,1)S(1)}, bf16[704,384]{1,0:T(8,128)(2,1)}, u32[]{:S(2)}, u32[]{:S(2)}) %collective-permute-start.13) | collective-permute-done | bytes 540704 | tf_op jit(solution)/shard_map/ppermute | solution.py:26
  60.3 1.7 slice.115
  61.9 4.6 %collective-permute-start.15 = (bf16[352,384]{1,0:T(8,128)(2,1)}, bf16[352,384]{1,0:T(8,128)(2,1)}, u32[]{:S(2)}, u32[]{:S(2)}) collective-permute-start(bf16[352,384]{1,0:T(8,128)(2,1)} %slice.115), channel_id=1, source_target_pairs={{0,12},{1,13},{2,14},{3,15},{4,0},{5,1},{6,2},{7,3},{8,4},{9,5},{1... | collective-permute-start | bytes 811016 | tf_op jit(solution)/shard_map/ppermute | solution.py:26
  66.5 1.7 slice.114
  68.2 8.9 %collective-permute-done.9.refs_2_ = bf16[1856,384]{1,0:T(8,128)(2,1)S(1)} collective-permute-done((bf16[1856,384]{1,0:T(8,128)(2,1)}, bf16[1856,384]{1,0:T(8,128)(2,1)S(1)}, u32[]{:S(2)}, u32[]{:S(2)}) %collective-permute-start.9) | collective-permute-done | bytes 1425440 | tf_op jit(solution)/shard_map/ppermute | solution.py:26
  77.1 1.0 slice.113
  78.1 3.0 collective-permute-start.11
  81.1 1.0 slice.112
  82.1 1.2 bitcast_select_fusion.cot_ref
  83.5 7.5 %collective-permute-done.11.refs_4_ = bf16[928,384]{1,0:T(8,128)(2,1)} collective-permute-done((bf16[928,384]{1,0:T(8,128)(2,1)}, bf16[928,384]{1,0:T(8,128)(2,1)}, u32[]{:S(2)}, u32[]{:S(2)}) %collective-permute-start.11) | collective-permute-done | bytes 712736 | tf_op jit(solution)/shard_map/ppermute | solution.py:26
  90.9 4.2 %collective-permute-done.10.refs_3_ = bf16[928,384]{1,0:T(8,128)(2,1)} collective-permute-done((bf16[928,384]{1,0:T(8,128)(2,1)}, bf16[928,384]{1,0:T(8,128)(2,1)}, u32[]{:S(2)}, u32[]{:S(2)}) %collective-permute-start.10) | collective-permute-done | bytes 712736 | tf_op jit(solution)/shard_map/ppermute | solution.py:26
  95.1 16.1 %shard_map.129 = (bf16[128,5120]{1,0:T(8,128)(2,1)}, bf16[4,2,320,384]{3,2,1,0:T(8,128)(2,1)}, bf16[2,4,2,160,384]{4,3,2,1,0:T(8,128)(2,1)}, bf16[2,4,2,160,384]...) custom-call(s32[2]{0:T(128)S(1)} %pad_add_fusion.where_ref, ...), custom_call_target="tpu_custom_call" | custom-call | flops 24999999488 | bytes 75000000 | tf_op jit(solution)/shard_map/pallas_call | solution.py:424
  111.2 9.0 %collective-permute-start.16 = (bf16[128,5120]{1,0:T(8,128)(2,1)}, bf16[128,5120]{1,0:T(8,128)(2,1)S(1)}, u32[]{:S(2)}, u32[]{:S(2)}) collective-permute-start(bf16[128,5120]{1,0:T(8,128)(2,1)} %get-tuple-element.36), channel_id=1, source_target_pairs={{16,0},{17,1},{18,2},{19,3},{20,4},{21,5},{22,6},{23,7},{24,8},{25... | collective-permute-start | bytes 3932168 | tf_op jit(solution)/shard_map/ppermute | solution.py:26
  120.3 10.1 %shard_map.130 = bf16[128,5120]{1,0:T(8,128)(2,1)S(1)} custom-call(s32[2]{0:T(128)S(1)} %pad_add_fusion.where_ref, f32[2,5120]{1,0:T(2,128)S(1)} %bitcast.65, bf16[128,5120]{1,0:T(8,128)(2,1)S(1)} %bitcast.63, bf16[1856,384]{1,0:T(8,128)(2,1)} %constant_dynamic-update-slice_fusion.refs_0_, bf16[1856,384]{1,0:T(8,128)(2,1)S(1)} %copy-done.3, ...), custom_call_target="tpu_custom_call" | custom-call | flops 12000000000 | bytes 36000000 | tf_op jit(solution)/shard_map/pallas_call | solution.py:446
  130.4 9.3 %collective-permute-done.16.rows_ref = bf16[128,5120]{1,0:T(8,128)(2,1)S(1)} collective-permute-done((bf16[128,5120]{1,0:T(8,128)(2,1)}, bf16[128,5120]{1,0:T(8,128)(2,1)S(1)}, u32[]{:S(2)}, u32[]{:S(2)}) %collective-permute-start.16) | collective-permute-done | bytes 1310752 | tf_op jit(solution)/shard_map/ppermute | solution.py:26
  139.7 2.4 shard_map.132
  142.1 4.5 %all-to-all-start.1 = ((bf16[16,16,5120]{2,1,0:T(8,128)(2,1)}), bf16[16,16,5120]{2,1,0:T(8,128)(2,1)}, u32[]{:S(2)}, u32[]{:S(2)}) async-start(bf16[16,16,5120]{2,1,0:T(8,128)(2,1)} %shard_map.132), calls=%async_computation.1 | async-start | bytes 5242880 | tf_op jit(solution)/shard_map/all_to_all | solution.py:301
  146.5 1.2 collective-permute-start.18
  147.7 1.6 collective-permute-start.19
  149.3 2.4 collective-permute-start.17
  151.7 63.0 %collective-permute-done.17.rows_ref = bf16[128,5120]{1,0:T(8,128)(2,1)S(1)} collective-permute-done((bf16[128,5120]{1,0:T(8,128)(2,1)S(1)}, bf16[128,5120]{1,0:T(8,128)(2,1)S(1)}, u32[]{:S(2)}, u32[]{:S(2)}) %collective-permute-start.17) | collective-permute-done | bytes 1310752 | tf_op jit(solution)/shard_map/ppermute | solution.py:26
  214.7 2.4 shard_map.131
  217.1 1.0 collective-permute-done.18
  218.1 7.7 %all-to-all-start = ((bf16[16,16,5120]{2,1,0:T(8,128)(2,1)}), bf16[16,16,5120]{2,1,0:T(8,128)(2,1)S(1)}, u32[]{:S(2)}, u32[]{:S(2)}) async-start(bf16[16,16,5120]{2,1,0:T(8,128)(2,1)} %shard_map.131), calls=%async_computation | async-start | bytes 5242880 | tf_op jit(solution)/shard_map/all_to_all | solution.py:301
  225.8 2.7 fusion.2
  228.6 1.4 collective-permute-start.20
  230.0 1.3 collective-permute-start.21
  231.3 30.1 %collective-permute-done.20 = bf16[4,2,160,384]{3,2,1,0:T(8,128)(2,1)S(1)} collective-permute-done((bf16[4,2,160,384]{3,2,1,0:T(8,128)(2,1)S(1)}, bf16[4,2,160,384]{3,2,1,0:T(8,128)(2,1)S(1)}, u32[]{:S(2)}, u32[]{:S(2)}) %collective-permute-start.20) | collective-permute-done | bytes 983072 | tf_op jit(solution)/shard_map/ppermute | solution.py:26
  261.4 2.3 fusion.1
  263.8 1.1 pad_maximum_fusion.1
  265.2 5.3 %collective-permute-start.22 = (bf16[2,2,160,384]{3,2,1,0:T(8,128)(2,1)}, bf16[2,2,160,384]{3,2,1,0:T(8,128)(2,1)S(1)}, u32[]{:S(2)}, u32[]{:S(2)}) collective-permute-start(bf16[2,2,160,384]{3,2,1,0:T(8,128)(2,1)} %pad_maximum_fusion.1), channel_id=1, source_target_pairs={{0,4},{1,5},{2,6},{3,7},{4,8},{5,9},{6,10},{7,11},{8,12},{9,13},{1... | collective-permute-start | bytes 1474568 | tf_op jit(solution)/shard_map/ppermute | solution.py:26
  270.5 0.8 pad_maximum_fusion.2
  271.3 3.5 %collective-permute-start.23 = (bf16[2,2,160,384]{3,2,1,0:T(8,128)(2,1)}, bf16[2,2,160,384]{3,2,1,0:T(8,128)(2,1)}, u32[]{:S(2)}, u32[]{:S(2)}) collective-permute-start(bf16[2,2,160,384]{3,2,1,0:T(8,128)(2,1)} %pad_maximum_fusion.2), channel_id=1, source_target_pairs={{0,12},{1,13},{2,14},{3,15},{4,0},{5,1},{6,2},{7,3},{8,4},{9,5},{1... | collective-permute-start | bytes 1474568 | tf_op jit(solution)/shard_map/ppermute | solution.py:26
  274.8 5.9 %shard_map.133 = bf16[16,16,5120]{2,1,0:T(8,128)(2,1)} custom-call(bf16[16,16,5120]{2,1,0:T(8,128)(2,1)} %all-to-all-done.1.from_ref), custom_call_target="tpu_custom_call" | custom-call | flops 3000000000 | bytes 9000000 | tf_op jit(solution)/shard_map/pallas_call | solution.py:310
  280.6 17.2 %collective-permute-done.22 = bf16[2,2,160,384]{3,2,1,0:T(8,128)(2,1)S(1)} collective-permute-done((bf16[2,2,160,384]{3,2,1,0:T(8,128)(2,1)}, bf16[2,2,160,384]{3,2,1,0:T(8,128)(2,1)S(1)}, u32[]{:S(2)}, u32[]{:S(2)}) %collective-permute-start.22) | collective-permute-done | bytes 491552 | tf_op jit(solution)/shard_map/ppermute | solution.py:26
  297.8 2.7 collective-permute-done.23
  300.5 1.0 fusion.7
  301.5 1.1 fusion.8
  302.6 11.1 %collective-permute-start.24 = (bf16[2,160,384]{2,1,0:T(8,128)(2,1)S(1)}, bf16[2,160,384]{2,1,0:T(8,128)(2,1)S(1)}, u32[]{:S(2)}, u32[]{:S(2)}) collective-permute-start(bf16[2,160,384]{2,1,0:T(8,128)(2,1)S(1)} %fusion.7), channel_id=1, source_target_pairs={{0,4},{1,5},{2,6},{3,7},{4,8},{5,9},{6,10},{7,11},{8,12},{9,13},{1... | collective-permute-start | bytes 737288 | tf_op jit(solution)/shard_map/ppermute | solution.py:26
  313.7 10.1 %collective-permute-done.24 = bf16[2,160,384]{2,1,0:T(8,128)(2,1)S(1)} collective-permute-done((bf16[2,160,384]{2,1,0:T(8,128)(2,1)S(1)}, bf16[2,160,384]{2,1,0:T(8,128)(2,1)S(1)}, u32[]{:S(2)}, u32[]{:S(2)}) %collective-permute-start.24) | collective-permute-done | bytes 245792 | tf_op jit(solution)/shard_map/ppermute | solution.py:26
  323.8 1.1 convert_add_fusion.6
  324.9 1.3 collective-permute-done.25
  326.3 1.0 convert_add_fusion.4
  327.3 0.7 fusion.6
  328.0 0.9 fusion.5
  328.9 1.5 copy.19
  (61 shorter events, 1.6 us)
Async XLA Ops:
  0.6 6.5 %copy-start.10 = (bf16[1,2,128,320]{2,3,1,0:T(8,128)(2,1)S(1)}, bf16[1,2,128,320]{2,3,1,0:T(8,128)(2,1)}, u32[]{:S(2)}) copy-start(bf16[1,2,128,320]{2,3,1,0:T(8,128)(2,1)} %param.19) | copy-start | bytes 491524
  0.6 6.5 %copy-start.8 = (bf16[1,2,320,256]{3,2,1,0:T(8,128)(2,1)S(1)}, bf16[1,2,320,256]{3,2,1,0:T(8,128)(2,1)}, u32[]{:S(2)}) copy-start(bf16[1,2,320,256]{3,2,1,0:T(8,128)(2,1)} %param.18) | copy-start | bytes 983044
  0.7 13.8 %copy-start.13 = (s32[16]{0:T(128)S(1)}, s32[16]{0:T(128)}, u32[]{:S(2)}) copy-start(s32[16]{0:T(128)} %param.14) | copy-start | bytes 196
  0.7 15.1 %copy-start.14 = (s32[1,1,8]{2,1,0:T(1,128)S(1)}, s32[1,1,8]{2,1,0:T(1,128)}, u32[]{:S(2)}) copy-start(s32[1,1,8]{2,1,0:T(1,128)} %param.16) | copy-start | bytes 100
  0.7 15.2 %copy-start.15 = (s32[1,1,8]{2,1,0:T(1,128)S(1)}, s32[1,1,8]{2,1,0:T(1,128)}, u32[]{:S(2)}) copy-start(s32[1,1,8]{2,1,0:T(1,128)} %param.15) | copy-start | bytes 100
  4.0 23.0 %collective-permute-start = (bf16[464,384]{1,0:T(8,128)(2,1)S(1)}, bf16[464,384]{1,0:T(8,128)(2,1)S(1)}, u32[]{:S(2)}, u32[]{:S(2)}) collective-permute-start(bf16[464,384]{1,0:T(8,128)(2,1)S(1)} %pad_maximum_fusion.3), channel_id=1, source_target_pairs={{0,4},{1,5},{2,6},{3,7},{4,8},{5,9},{6,10},{7,11},{8,12},{9,13},{1... | collective-permute-start | bytes 1069064 | tf_op jit(solution)/shard_map/ppermute | solution.py:26
  7.1 8.8 %collective-permute-start.5 = (bf16[176,384]{1,0:T(8,128)(2,1)S(1)}, bf16[176,384]{1,0:T(8,128)(2,1)S(1)}, u32[]{:S(2)}, u32[]{:S(2)}) collective-permute-start(bf16[176,384]{1,0:T(8,128)(2,1)S(1)} %fusion.11), channel_id=1, source_target_pairs={{0,2},{1,3},{2,0},{3,1},{4,6},{5,7},{6,4},{7,5},{8,10},{9,11},{10,... | collective-permute-start | bytes 405512 | tf_op jit(solution)/shard_map/ppermute | solution.py:26
  10.0 10.5 %collective-permute-start.4 = (bf16[176,384]{1,0:T(8,128)(2,1)S(1)}, bf16[176,384]{1,0:T(8,128)(2,1)S(1)}, u32[]{:S(2)}, u32[]{:S(2)}) collective-permute-start(bf16[176,384]{1,0:T(8,128)(2,1)S(1)} %fusion.11), channel_id=1, source_target_pairs={{0,3},{1,0},{2,1},{3,2},{4,7},{5,4},{6,5},{7,6},{8,11},{9,8},{10,9... | collective-permute-start | bytes 405512 | tf_op jit(solution)/shard_map/ppermute | solution.py:26
  10.8 14.2 %collective-permute-start.3 = (bf16[176,384]{1,0:T(8,128)(2,1)S(1)}, bf16[176,384]{1,0:T(8,128)(2,1)S(1)}, u32[]{:S(2)}, u32[]{:S(2)}) collective-permute-start(bf16[176,384]{1,0:T(8,128)(2,1)S(1)} %fusion.11), channel_id=1, source_target_pairs={{0,1},{1,2},{2,3},{3,0},{4,5},{5,6},{6,7},{7,4},{8,9},{9,10},{10,1... | collective-permute-start | bytes 405512 | tf_op jit(solution)/shard_map/ppermute | solution.py:26
  11.4 29.1 %collective-permute-start.1 = (bf16[464,384]{1,0:T(8,128)(2,1)S(1)}, bf16[464,384]{1,0:T(8,128)(2,1)S(1)}, u32[]{:S(2)}, u32[]{:S(2)}) collective-permute-start(bf16[464,384]{1,0:T(8,128)(2,1)S(1)} %pad_maximum_fusion.3), channel_id=1, source_target_pairs={{0,12},{1,13},{2,14},{3,15},{4,0},{5,1},{6,2},{7,3},{8,4},{9,5},{1... | collective-permute-start | bytes 1069064 | tf_op jit(solution)/shard_map/ppermute | solution.py:26
  15.9 34.9 %copy-start.12 = (s32[1,1,8]{2,1,0:T(1,128)S(1)}, s32[1,1,8]{2,1,0:T(1,128)}, u32[]{:S(2)}) copy-start(s32[1,1,8]{2,1,0:T(1,128)} %param.13) | copy-start | bytes 100
  15.9 25.4 %collective-permute-start.2 = (bf16[464,384]{1,0:T(8,128)(2,1)S(1)}, bf16[464,384]{1,0:T(8,128)(2,1)S(1)}, u32[]{:S(2)}, u32[]{:S(2)}) collective-permute-start(bf16[464,384]{1,0:T(8,128)(2,1)S(1)} %pad_maximum_fusion.3), channel_id=1, source_target_pairs={{0,8},{1,9},{2,10},{3,11},{4,12},{5,13},{6,14},{7,15},{8,0},{9,1},... | collective-permute-start | bytes 1069064 | tf_op jit(solution)/shard_map/ppermute | solution.py:26
  20.5 21.6 %collective-permute-start.6 = (s32[16]{0:T(128)S(1)}, s32[16]{0:T(128)S(1)}, u32[]{:S(2)}, u32[]{:S(2)}) collective-permute-start(s32[16]{0:T(128)S(1)} %select_reduce_fusion.1), channel_id=1, source_target_pairs={{0,16},{1,17},{2,18},{3,19},{4,20},{5,21},{6,22},{7,23},{8,24},{9,... | collective-permute-start | bytes 200 | tf_op jit(solution)/shard_map/ppermute | solution.py:26
  25.0 21.3 %collective-permute-start.7 = (s32[16]{0:T(128)S(1)}, s32[16]{0:T(128)S(1)}, u32[]{:S(2)}, u32[]{:S(2)}) collective-permute-start(s32[16]{0:T(128)S(1)} %select_reduce_fusion), channel_id=1, source_target_pairs={{16,0},{17,1},{18,2},{19,3},{20,4},{21,5},{22,6},{23,7},{24,8},{25... | collective-permute-start | bytes 200 | tf_op jit(solution)/shard_map/ppermute | solution.py:26
  46.4 30.7 %collective-permute-start.9 = (bf16[1856,384]{1,0:T(8,128)(2,1)}, bf16[1856,384]{1,0:T(8,128)(2,1)S(1)}, u32[]{:S(2)}, u32[]{:S(2)}) collective-permute-start(bf16[1856,384]{1,0:T(8,128)(2,1)} %constant_dynamic-update-slice_fusion.refs_0_), channel_id=1, source_target_pairs={{0,3},{1,0},{2,1},{3,2},{4,7},{5,4},{6,5},{7,6},{8,11},{9,8},{10,9... | collective-permute-start | bytes 4276232 | tf_op jit(solution)/shard_map/ppermute | solution.py:26
  48.4 32.6 %collective-permute-start.8 = (bf16[1856,384]{1,0:T(8,128)(2,1)}, bf16[1856,384]{1,0:T(8,128)(2,1)S(1)}, u32[]{:S(2)}, u32[]{:S(2)}) collective-permute-start(bf16[1856,384]{1,0:T(8,128)(2,1)} %constant_dynamic-update-slice_fusion.refs_0_), channel_id=1, source_target_pairs={{0,1},{1,2},{2,3},{3,0},{4,5},{5,6},{6,7},{7,4},{8,9},{9,10},{10,1... | collective-permute-start | bytes 4276232 | tf_op jit(solution)/shard_map/ppermute | solution.py:26
  48.4 11.8 %collective-permute-start.13 = (bf16[704,384]{1,0:T(8,128)(2,1)S(1)}, bf16[704,384]{1,0:T(8,128)(2,1)}, u32[]{:S(2)}, u32[]{:S(2)}) collective-permute-start(bf16[704,384]{1,0:T(8,128)(2,1)S(1)} %pad_maximum_fusion.refs_5_), channel_id=1, source_target_pairs={{0,12},{1,13},{2,14},{3,15},{4,0},{5,1},{6,2},{7,3},{8,4},{9,5},{1... | collective-permute-start | bytes 1622024 | tf_op jit(solution)/shard_map/ppermute | solution.py:26
  49.0 17.5 %collective-permute-start.12 = (bf16[704,384]{1,0:T(8,128)(2,1)S(1)}, bf16[704,384]{1,0:T(8,128)(2,1)}, u32[]{:S(2)}, u32[]{:S(2)}) collective-permute-start(bf16[704,384]{1,0:T(8,128)(2,1)S(1)} %pad_maximum_fusion.refs_5_), channel_id=1, source_target_pairs={{0,4},{1,5},{2,6},{3,7},{4,8},{5,9},{6,10},{7,11},{8,12},{9,13},{1... | collective-permute-start | bytes 1622024 | tf_op jit(solution)/shard_map/ppermute | solution.py:26
  61.9 21.5 %collective-permute-start.15 = (bf16[352,384]{1,0:T(8,128)(2,1)}, bf16[352,384]{1,0:T(8,128)(2,1)}, u32[]{:S(2)}, u32[]{:S(2)}) collective-permute-start(bf16[352,384]{1,0:T(8,128)(2,1)} %slice.115), channel_id=1, source_target_pairs={{0,12},{1,13},{2,14},{3,15},{4,0},{5,1},{6,2},{7,3},{8,4},{9,5},{1... | collective-permute-start | bytes 811016 | tf_op jit(solution)/shard_map/ppermute | solution.py:26
  68.2 13.9 %copy-start.11 = (bf16[1,1,8,16,5120]{4,3,2,1,0:T(8,128)(2,1)S(1)}, bf16[1,1,8,16,5120]{4,3,2,1,0:T(8,128)(2,1)}, u32[]{:S(2)}) copy-start(bf16[1,1,8,16,5120]{4,3,2,1,0:T(8,128)(2,1)} %param.12) | copy-start | bytes 3932164
  68.2 15.3 %collective-permute-start.14 = (bf16[352,384]{1,0:T(8,128)(2,1)}, bf16[352,384]{1,0:T(8,128)(2,1)}, u32[]{:S(2)}, u32[]{:S(2)}) collective-permute-start(bf16[352,384]{1,0:T(8,128)(2,1)} %slice.114), channel_id=1, source_target_pairs={{0,4},{1,5},{2,6},{3,7},{4,8},{5,9},{6,10},{7,11},{8,12},{9,13},{1... | collective-permute-start | bytes 811016 | tf_op jit(solution)/shard_map/ppermute | solution.py:26
  77.1 5.0 %copy-start = (bf16[1856,384]{1,0:T(8,128)(2,1)}, bf16[1856,384]{1,0:T(8,128)(2,1)S(1)}, u32[]{:S(2)}) copy-start(bf16[1856,384]{1,0:T(8,128)(2,1)S(1)} %collective-permute-done.9.refs_2_) | copy-start | bytes 4276228
  78.1 12.8 %collective-permute-start.11 = (bf16[928,384]{1,0:T(8,128)(2,1)}, bf16[928,384]{1,0:T(8,128)(2,1)}, u32[]{:S(2)}, u32[]{:S(2)}) collective-permute-start(bf16[928,384]{1,0:T(8,128)(2,1)} %slice.113), channel_id=1, source_target_pairs={{0,3},{1,0},{2,1},{3,2},{4,7},{5,4},{6,5},{7,6},{8,11},{9,8},{10,9... | collective-permute-start | bytes 2138120 | tf_op jit(solution)/shard_map/ppermute | solution.py:26
  81.1 2.3 copy-start.2
  82.1 13.0 %copy-start.5 = (f32[1,2,5120]{2,1,0:T(2,128)S(1)}, f32[1,2,5120]{2,1,0:T(2,128)}, u32[]{:S(2)}) copy-start(f32[1,2,5120]{2,1,0:T(2,128)} %param.17) | copy-start | bytes 122884
  82.1 13.0 %collective-permute-start.10 = (bf16[928,384]{1,0:T(8,128)(2,1)}, bf16[928,384]{1,0:T(8,128)(2,1)}, u32[]{:S(2)}, u32[]{:S(2)}) collective-permute-start(bf16[928,384]{1,0:T(8,128)(2,1)} %slice.112), channel_id=1, source_target_pairs={{0,1},{1,2},{2,3},{3,0},{4,5},{5,6},{6,7},{7,4},{8,9},{9,10},{10,1... | collective-permute-start | bytes 2138120 | tf_op jit(solution)/shard_map/ppermute | solution.py:26
  95.1 25.1 %copy-start.1 = (bf16[1856,384]{1,0:T(8,128)(2,1)S(1)}, bf16[1856,384]{1,0:T(8,128)(2,1)}, u32[]{:S(2)}) copy-start(bf16[1856,384]{1,0:T(8,128)(2,1)} %copy-done) | copy-start | bytes 4276228
  95.1 25.1 %copy-start.3 = (bf16[1856,384]{1,0:T(8,128)(2,1)S(1)}, bf16[1856,384]{1,0:T(8,128)(2,1)}, u32[]{:S(2)}) copy-start(bf16[1856,384]{1,0:T(8,128)(2,1)} %copy-done.2) | copy-start | bytes 4276228
  95.1 25.1 %copy-start.4 = (bf16[1,1,8,16,5120]{4,3,2,1,0:T(8,128)(2,1)S(1)}, bf16[1,1,8,16,5120]{4,3,2,1,0:T(8,128)(2,1)}, u32[]{:S(2)}) copy-start(bf16[1,1,8,16,5120]{4,3,2,1,0:T(8,128)(2,1)} %param.10) | copy-start | bytes 3932164
  111.2 28.5 %collective-permute-start.16 = (bf16[128,5120]{1,0:T(8,128)(2,1)}, bf16[128,5120]{1,0:T(8,128)(2,1)S(1)}, u32[]{:S(2)}, u32[]{:S(2)}) collective-permute-start(bf16[128,5120]{1,0:T(8,128)(2,1)} %get-tuple-element.36), channel_id=1, source_target_pairs={{16,0},{17,1},{18,2},{19,3},{20,4},{21,5},{22,6},{23,7},{24,8},{25... | collective-permute-start | bytes 3932168 | tf_op jit(solution)/shard_map/ppermute | solution.py:26
  142.1 76.0 %all-to-all-start.1 = ((bf16[16,16,5120]{2,1,0:T(8,128)(2,1)}), bf16[16,16,5120]{2,1,0:T(8,128)(2,1)}, u32[]{:S(2)}, u32[]{:S(2)}) async-start(bf16[16,16,5120]{2,1,0:T(8,128)(2,1)} %shard_map.132), calls=%async_computation.1 | async-start | bytes 5242880 | tf_op jit(solution)/shard_map/all_to_all | solution.py:301
  146.5 71.6 %collective-permute-start.18 = (bf16[2,4,2,160,384]{4,3,2,1,0:T(8,128)(2,1)}, bf16[2,4,2,160,384]{4,3,2,1,0:T(8,128)(2,1)}, u32[]{:S(2)}, u32[]{:S(2)}) collective-permute-start(bf16[2,4,2,160,384]{4,3,2,1,0:T(8,128)(2,1)} %get-tuple-element.39), channel_id=1, source_target_pairs={{0,1},{1,2},{2,3},{3,0},{4,5},{5,6},{6,7},{7,4},{8,9},{9,10},{10,1... | collective-permute-start | bytes 5898248 | tf_op jit(solution)/shard_map/ppermute | solution.py:26
  147.7 70.4 %collective-permute-start.19 = (bf16[2,4,2,160,384]{4,3,2,1,0:T(8,128)(2,1)}, bf16[2,4,2,160,384]{4,3,2,1,0:T(8,128)(2,1)}, u32[]{:S(2)}, u32[]{:S(2)}) collective-permute-start(bf16[2,4,2,160,384]{4,3,2,1,0:T(8,128)(2,1)} %get-tuple-element.40), channel_id=1, source_target_pairs={{0,3},{1,0},{2,1},{3,2},{4,7},{5,4},{6,5},{7,6},{8,11},{9,8},{10,9... | collective-permute-start | bytes 5898248 | tf_op jit(solution)/shard_map/ppermute | solution.py:26
  149.3 65.4 %collective-permute-start.17 = (bf16[128,5120]{1,0:T(8,128)(2,1)S(1)}, bf16[128,5120]{1,0:T(8,128)(2,1)S(1)}, u32[]{:S(2)}, u32[]{:S(2)}) collective-permute-start(bf16[128,5120]{1,0:T(8,128)(2,1)S(1)} %shard_map.130), channel_id=1, source_target_pairs={{0,16},{1,17},{2,18},{3,19},{4,20},{5,21},{6,22},{7,23},{8,24},{9,... | collective-permute-start | bytes 3932168 | tf_op jit(solution)/shard_map/ppermute | solution.py:26
  218.1 110.8 %all-to-all-start = ((bf16[16,16,5120]{2,1,0:T(8,128)(2,1)}), bf16[16,16,5120]{2,1,0:T(8,128)(2,1)S(1)}, u32[]{:S(2)}, u32[]{:S(2)}) async-start(bf16[16,16,5120]{2,1,0:T(8,128)(2,1)} %shard_map.131), calls=%async_computation | async-start | bytes 5242880 | tf_op jit(solution)/shard_map/all_to_all | solution.py:301
  225.8 35.6 %copy-start.9 = (bf16[4,2,320,384]{3,2,1,0:T(8,128)(2,1)S(1)}, bf16[4,2,320,384]{3,2,1,0:T(8,128)(2,1)}, u32[]{:S(2)}) copy-start(bf16[4,2,320,384]{3,2,1,0:T(8,128)(2,1)} %get-tuple-element.42) | copy-start | bytes 5898244
  228.6 32.9 %collective-permute-start.20 = (bf16[4,2,160,384]{3,2,1,0:T(8,128)(2,1)S(1)}, bf16[4,2,160,384]{3,2,1,0:T(8,128)(2,1)S(1)}, u32[]{:S(2)}, u32[]{:S(2)}) collective-permute-start(bf16[4,2,160,384]{3,2,1,0:T(8,128)(2,1)S(1)} %get-tuple-element.47), channel_id=1, source_target_pairs={{0,1},{1,2},{2,3},{3,0},{4,5},{5,6},{6,7},{7,4},{8,9},{9,10},{10,1... | collective-permute-start | bytes 2949128 | tf_op jit(solution)/shard_map/ppermute | solution.py:26
  230.0 31.4 %collective-permute-start.21 = (bf16[4,2,160,384]{3,2,1,0:T(8,128)(2,1)S(1)}, bf16[4,2,160,384]{3,2,1,0:T(8,128)(2,1)S(1)}, u32[]{:S(2)}, u32[]{:S(2)}) collective-permute-start(bf16[4,2,160,384]{3,2,1,0:T(8,128)(2,1)S(1)} %get-tuple-element.48), channel_id=1, source_target_pairs={{0,3},{1,0},{2,1},{3,2},{4,7},{5,4},{6,5},{7,6},{8,11},{9,8},{10,9... | collective-permute-start | bytes 2949128 | tf_op jit(solution)/shard_map/ppermute | solution.py:26
  263.7 1.2 copy-start.6
  263.7 1.5 copy-start.7
  265.2 32.6 %collective-permute-start.22 = (bf16[2,2,160,384]{3,2,1,0:T(8,128)(2,1)}, bf16[2,2,160,384]{3,2,1,0:T(8,128)(2,1)S(1)}, u32[]{:S(2)}, u32[]{:S(2)}) collective-permute-start(bf16[2,2,160,384]{3,2,1,0:T(8,128)(2,1)} %pad_maximum_fusion.1), channel_id=1, source_target_pairs={{0,4},{1,5},{2,6},{3,7},{4,8},{5,9},{6,10},{7,11},{8,12},{9,13},{1... | collective-permute-start | bytes 1474568 | tf_op jit(solution)/shard_map/ppermute | solution.py:26
  271.3 29.2 %collective-permute-start.23 = (bf16[2,2,160,384]{3,2,1,0:T(8,128)(2,1)}, bf16[2,2,160,384]{3,2,1,0:T(8,128)(2,1)}, u32[]{:S(2)}, u32[]{:S(2)}) collective-permute-start(bf16[2,2,160,384]{3,2,1,0:T(8,128)(2,1)} %pad_maximum_fusion.2), channel_id=1, source_target_pairs={{0,12},{1,13},{2,14},{3,15},{4,0},{5,1},{6,2},{7,3},{8,4},{9,5},{1... | collective-permute-start | bytes 1474568 | tf_op jit(solution)/shard_map/ppermute | solution.py:26
  302.6 21.1 %collective-permute-start.24 = (bf16[2,160,384]{2,1,0:T(8,128)(2,1)S(1)}, bf16[2,160,384]{2,1,0:T(8,128)(2,1)S(1)}, u32[]{:S(2)}, u32[]{:S(2)}) collective-permute-start(bf16[2,160,384]{2,1,0:T(8,128)(2,1)S(1)} %fusion.7), channel_id=1, source_target_pairs={{0,4},{1,5},{2,6},{3,7},{4,8},{5,9},{6,10},{7,11},{8,12},{9,13},{1... | collective-permute-start | bytes 737288 | tf_op jit(solution)/shard_map/ppermute | solution.py:26
  313.7 12.5 %collective-permute-start.25 = (bf16[2,160,384]{2,1,0:T(8,128)(2,1)S(1)}, bf16[2,160,384]{2,1,0:T(8,128)(2,1)S(1)}, u32[]{:S(2)}, u32[]{:S(2)}) collective-permute-start(bf16[2,160,384]{2,1,0:T(8,128)(2,1)S(1)} %fusion.8), channel_id=1, source_target_pairs={{0,12},{1,13},{2,14},{3,15},{4,0},{5,1},{6,2},{7,3},{8,4},{9,5},{1... | collective-permute-start | bytes 737288 | tf_op jit(solution)/shard_map/ppermute | solution.py:26

commit v3 on v2

--- a/solution.py
+++ b/solution.py
@@ -409,6 +409,18 @@
     anywhere = [pl.BlockSpec(memory_space=pl.ANY)] * len(spans)
     wide = [pltpu.VMEM((width, 3 * rank), bf16)] * 2
     sems = pltpu.SemaphoreType.DMA((sum(len(held) for held in spans),))
+    rows = pl.pallas_call(
+        functools.partial(forward_kernel, spans, share),
+        out_shape=flat,
+        in_specs=smem(1) + vmem(2) + anywhere,
+        out_specs=vmem(1)[0],
+        scratch_shapes=wide + [pltpu.VMEM((count, width), f32), sems],
+        compiler_params=pltpu.CompilerParams(vmem_limit_bytes=40 << 20),
+        cost_estimate=cost(12),
+    )(where, gains, forward_inputs.reshape(count, width), *arrays)
+
+    rows, saved = lax.optimization_barrier((rows, saved))
+
     def spread(index, rows):
         return pl.pallas_call(
             functools.partial(spread_kernel, slots),
@@ -418,6 +430,8 @@
             compiler_params=pltpu.CompilerParams(vmem_limit_bytes=16 << 20),
             cost_estimate=cost(2),
         )(index, rows)
+
+    shifted = move(rows, 0, 0, 1)
 
     part = shaped(ROW, 2, share // 2, 3 * rank)
     pair = shaped(2, ROW, 2, share // 2, 3 * rank)
@@ -438,27 +452,13 @@
         compiler_params=pltpu.CompilerParams(vmem_limit_bytes=52 << 20),
         cost_estimate=cost(25),
     )(where, gains, saved, cot, *arrays)
-    d_rows, up, down, inputs = lax.optimization_barrier(
-        (d_rows, up, down, forward_inputs.reshape(count, width))
-    )
+    shifted, d_rows, up, down = lax.optimization_barrier((shifted, d_rows, up, down))
     got_up, got_down = scatter_first(up, down, "x")
-    shifted = move(d_rows, 0, 0, -1)
-    rows = pl.pallas_call(
-        functools.partial(forward_kernel, spans, share),
-        out_shape=flat,
-        in_specs=smem(1) + vmem(2) + anywhere,
-        out_specs=vmem(1)[0],
-        scratch_shapes=wide + [pltpu.VMEM((count, width), f32), sems],
-        compiler_params=pltpu.CompilerParams(vmem_limit_bytes=40 << 20),
-        cost_estimate=cost(12),
-    )(where, gains, inputs, *arrays)
-
-    shifted, rows = lax.optimization_barrier((shifted, rows))
-    backward_arrived = settle(exchange(spread(back_slots, shifted)))
-    outgoing = spread(forward_slots, move(rows, 0, 0, 1))
-    outgoing, got_up, got_down = lax.optimization_barrier((outgoing, got_up, got_down))
-    forward_arrived = exchange(outgoing)
-    total, backward_arrived = reduce_scatter(own, ahead, behind, got_up, got_down, backward_arrived)
+    forward_arrived = settle(exchange(spread(forward_slots, shifted)))
+    returned = spread(back_slots, move(d_rows, 0, 0, -1))
+    returned, got_up, got_down = lax.optimization_barrier((returned, got_up, got_down))
+    backward_arrived = exchange(returned)
+    total, forward_arrived = reduce_scatter(own, ahead, behind, got_up, got_down, forward_arrived)
 
     grad_in = total[:, :, : 2 * rank]
     grad_down = jnp.swapaxes(total[:, :, 2 * rank :], 1, 2)

time: 332 us -> 334 us (level)
  the two profiles are of different devices: /device:TPU:25 before, /device:TPU:16 now
where the time goes in v3:
time: 334 us; the launch traced here: 333 us
  waiting for transfers between devices  186 us (56%)
  starting transfers between devices  76.2 us (23%)
  Pallas kernels  36.7 us (11%)
  other arithmetic  17.6 us (5%)
  local copies, waits for them, and re-layouts  14.5 us (4%)
    ppermute x26, waiting for transfers between devices, move(): return lax.ppermute(array, ('section', 'peer'), pairs)  186 us
    ppermute x26, starting transfers between devices, move(): return lax.ppermute(array, ('section', 'peer'), pairs)  62.6 us
    pallas_call x1, Pallas kernels, per_device(): pl.pallas_call(functools.partial(back_kernel, spans, share), out_shape=[f...  15.9 us
    all_to_all x2, starting transfers between devices, exchange(): lax.all_to_all(routed, 'peer', split_axis=0, concat_axis=0, tiled=True)  13.6 us
    pallas_call x1, Pallas kernels, per_device(): pl.pallas_call(functools.partial(forward_kernel, spans, share), out_shape...  10.1 us
    unnamed x37, local copies, waits for them, and re-layouts  7.51 us
  transfers between devices with their start and end apart: 28, of which 12 were waited for; matrix products, arithmetic and copies ran while one was open for 7% of the time, Pallas kernels for 7%

profile of v3, /device:TPU:16, one launch (start us, length us, event | category | flops | bytes accessed | tf_op | source)
XLA Modules:
  0.0 333.0 jit_solution(13221364583336153621)
XLA Ops:
  0.7 1.7 constant_dynamic-update-slice_fusion.4
  2.4 1.6 constant_dynamic-update-slice_fusion.3
  4.0 3.3 %collective-permute-start = (bf16[464,384]{1,0:T(8,128)(2,1)S(1)}, bf16[464,384]{1,0:T(8,128)(2,1)S(1)}, u32[]{:S(2)}, u32[]{:S(2)}) collective-permute-start(bf16[464,384]{1,0:T(8,128)(2,1)S(1)} %pad_maximum_fusion.3), channel_id=1, source_target_pairs={{0,4},{1,5},{2,6},{3,7},{4,8},{5,9},{6,10},{7,11},{8,12},{9,13},{1... | collective-permute-start | bytes 1069064 | tf_op jit(solution)/shard_map/ppermute | solution.py:26
  7.4 3.1 collective-permute-start.5
  10.5 1.1 collective-permute-start.4
  11.7 0.9 collective-permute-start.3
  12.6 3.1 collective-permute-start.1
  17.1 5.1 %collective-permute-start.2 = (bf16[464,384]{1,0:T(8,128)(2,1)S(1)}, bf16[464,384]{1,0:T(8,128)(2,1)S(1)}, u32[]{:S(2)}, u32[]{:S(2)}) collective-permute-start(bf16[464,384]{1,0:T(8,128)(2,1)S(1)} %pad_maximum_fusion.3), channel_id=1, source_target_pairs={{0,8},{1,9},{2,10},{3,11},{4,12},{5,13},{6,14},{7,15},{8,0},{9,1},... | collective-permute-start | bytes 1069064 | tf_op jit(solution)/shard_map/ppermute | solution.py:26
  22.1 1.9 collective-permute-start.6
  24.1 3.6 %collective-permute-start.7 = (s32[16]{0:T(128)S(1)}, s32[16]{0:T(128)S(1)}, u32[]{:S(2)}, u32[]{:S(2)}) collective-permute-start(s32[16]{0:T(128)S(1)} %select_reduce_fusion), channel_id=1, source_target_pairs={{16,0},{17,1},{18,2},{19,3},{20,4},{21,5},{22,6},{23,7},{24,8},{25... | collective-permute-start | bytes 200 | tf_op jit(solution)/shard_map/ppermute | solution.py:26
  27.8 0.8 constant_dynamic-update-slice_fusion.2
  28.6 12.3 %collective-permute-done.1 = bf16[464,384]{1,0:T(8,128)(2,1)S(1)} collective-permute-done((bf16[464,384]{1,0:T(8,128)(2,1)S(1)}, bf16[464,384]{1,0:T(8,128)(2,1)S(1)}, u32[]{:S(2)}, u32[]{:S(2)}) %collective-permute-start.1) | collective-permute-done | bytes 356384 | tf_op jit(solution)/shard_map/ppermute | solution.py:26
  42.5 2.4 collective-permute-start.9
  44.8 5.0 %collective-permute-start.13 = (bf16[704,384]{1,0:T(8,128)(2,1)S(1)}, bf16[704,384]{1,0:T(8,128)(2,1)}, u32[]{:S(2)}, u32[]{:S(2)}) collective-permute-start(bf16[704,384]{1,0:T(8,128)(2,1)S(1)} %pad_maximum_fusion.refs_5_), channel_id=1, source_target_pairs={{0,12},{1,13},{2,14},{3,15},{4,0},{5,1},{6,2},{7,3},{8,4},{9,5},{1... | collective-permute-start | bytes 1622024 | tf_op jit(solution)/shard_map/ppermute | solution.py:26
  49.8 5.1 %collective-permute-start.12 = (bf16[704,384]{1,0:T(8,128)(2,1)S(1)}, bf16[704,384]{1,0:T(8,128)(2,1)}, u32[]{:S(2)}, u32[]{:S(2)}) collective-permute-start(bf16[704,384]{1,0:T(8,128)(2,1)S(1)} %pad_maximum_fusion.refs_5_), channel_id=1, source_target_pairs={{0,4},{1,5},{2,6},{3,7},{4,8},{5,9},{6,10},{7,11},{8,12},{9,13},{1... | collective-permute-start | bytes 1622024 | tf_op jit(solution)/shard_map/ppermute | solution.py:26
  55.1 18.9 %collective-permute-done.13.refs_7_ = bf16[704,384]{1,0:T(8,128)(2,1)} collective-permute-done((bf16[704,384]{1,0:T(8,128)(2,1)S(1)}, bf16[704,384]{1,0:T(8,128)(2,1)}, u32[]{:S(2)}, u32[]{:S(2)}) %collective-permute-start.13) | collective-permute-done | bytes 540704 | tf_op jit(solution)/shard_map/ppermute | solution.py:26
  74.1 1.7 slice.115
  75.7 3.0 collective-permute-start.15
  78.8 1.7 slice.114
  80.5 3.9 %collective-permute-start.14 = (bf16[352,384]{1,0:T(8,128)(2,1)}, bf16[352,384]{1,0:T(8,128)(2,1)}, u32[]{:S(2)}, u32[]{:S(2)}) collective-permute-start(bf16[352,384]{1,0:T(8,128)(2,1)} %slice.114), channel_id=1, source_target_pairs={{0,4},{1,5},{2,6},{3,7},{4,8},{5,9},{6,10},{7,11},{8,12},{9,13},{1... | collective-permute-start | bytes 811016 | tf_op jit(solution)/shard_map/ppermute | solution.py:26
  84.3 1.1 slice.113
  85.4 1.1 collective-permute-start.11
  86.5 1.0 slice.112
  87.6 0.9 collective-permute-start.10
  88.5 1.3 bitcast_select_fusion.cot_ref
  89.9 5.2 %collective-permute-done.14.refs_8_ = bf16[352,384]{1,0:T(8,128)(2,1)} collective-permute-done((bf16[352,384]{1,0:T(8,128)(2,1)}, bf16[352,384]{1,0:T(8,128)(2,1)}, u32[]{:S(2)}, u32[]{:S(2)}) %collective-permute-start.14) | collective-permute-done | bytes 270368 | tf_op jit(solution)/shard_map/ppermute | solution.py:26
  95.1 2.9 collective-permute-done.11.refs_4_
  97.9 4.4 %collective-permute-done.10.refs_3_ = bf16[928,384]{1,0:T(8,128)(2,1)} collective-permute-done((bf16[928,384]{1,0:T(8,128)(2,1)}, bf16[928,384]{1,0:T(8,128)(2,1)}, u32[]{:S(2)}, u32[]{:S(2)}) %collective-permute-start.10) | collective-permute-done | bytes 712736 | tf_op jit(solution)/shard_map/ppermute | solution.py:26
  102.4 1.3 copy-done.2
  103.7 10.1 %shard_map.129 = bf16[128,5120]{1,0:T(8,128)(2,1)S(1)} custom-call(s32[2]{0:T(128)S(1)} %pad_add_fusion.where_ref, f32[2,5120]{1,0:T(2,128)S(1)} %bitcast.64, bf16[128,5120]{1,0:T(8,128)(2,1)S(1)} %bitcast.63, bf16[1856,384]{1,0:T(8,128)(2,1)} %constant_dynamic-update-slice_fusion.refs_0_, bf16[1856,384]{1,0:T(8,128)(2,1)S(1)} %collective-permute-done.8.refs_1_, ...), custom_call_target="tpu_custom_call" | custom-call | flops 12000000000 | bytes 36000000 | tf_op jit(solution)/shard_map/pallas_call | solution.py:412
  113.9 1.9 collective-permute-start.16
  115.8 15.9 %shard_map.130 = (bf16[128,5120]{1,0:T(8,128)(2,1)}, bf16[4,2,320,384]{3,2,1,0:T(8,128)(2,1)}, bf16[2,4,2,160,384]{4,3,2,1,0:T(8,128)(2,1)}, bf16[2,4,2,160,384]...) custom-call(s32[2]{0:T(128)S(1)} %pad_add_fusion.where_ref, ...), custom_call_target="tpu_custom_call" | custom-call | flops 24999999488 | bytes 75000000 | tf_op jit(solution)/shard_map/pallas_call | solution.py:438
  131.7 1.1 collective-permute-done.16.rows_ref
  132.8 2.4 shard_map.132
  135.2 5.3 %all-to-all-start = ((bf16[16,16,5120]{2,1,0:T(8,128)(2,1)}), bf16[16,16,5120]{2,1,0:T(8,128)(2,1)S(1)}, u32[]{:S(2)}, u32[]{:S(2)}) async-start(bf16[16,16,5120]{2,1,0:T(8,128)(2,1)} %shard_map.132), calls=%async_computation | async-start | bytes 5242880 | tf_op jit(solution)/shard_map/all_to_all | solution.py:301
  140.5 1.9 collective-permute-start.18
  142.4 1.4 collective-permute-start.19
  143.8 1.9 collective-permute-start.17
  145.7 15.4 %collective-permute-done.17.rows_ref = bf16[128,5120]{1,0:T(8,128)(2,1)S(1)} collective-permute-done((bf16[128,5120]{1,0:T(8,128)(2,1)}, bf16[128,5120]{1,0:T(8,128)(2,1)S(1)}, u32[]{:S(2)}, u32[]{:S(2)}) %collective-permute-start.17) | collective-permute-done | bytes 1310752 | tf_op jit(solution)/shard_map/ppermute | solution.py:26
  161.1 2.4 shard_map.131
  163.5 50.5 %collective-permute-done.18 = bf16[2,4,2,160,384]{4,3,2,1,0:T(8,128)(2,1)S(1)} collective-permute-done((bf16[2,4,2,160,384]{4,3,2,1,0:T(8,128)(2,1)}, bf16[2,4,2,160,384]{4,3,2,1,0:T(8,128)(2,1)S(1)}, u32[]{:S(2)}, u32[]{:S(2)}) %collective-permute-start.18) | collective-permute-done | bytes 1966112 | tf_op jit(solution)/shard_map/ppermute | solution.py:26
  214.1 1.3 copy-done.8
  215.4 1.5 copy-done.7
  216.9 8.3 %all-to-all-start.1 = ((bf16[16,16,5120]{2,1,0:T(8,128)(2,1)}), bf16[16,16,5120]{2,1,0:T(8,128)(2,1)S(1)}, u32[]{:S(2)}, u32[]{:S(2)}) async-start(bf16[16,16,5120]{2,1,0:T(8,128)(2,1)} %shard_map.131), calls=%async_computation.1 | async-start | bytes 5242880 | tf_op jit(solution)/shard_map/all_to_all | solution.py:301
  225.2 2.7 fusion.2
  227.9 2.2 collective-permute-start.20
  230.2 1.3 collective-permute-start.21
  231.5 46.5 %collective-permute-done.20 = bf16[4,2,160,384]{3,2,1,0:T(8,128)(2,1)S(1)} collective-permute-done((bf16[4,2,160,384]{3,2,1,0:T(8,128)(2,1)S(1)}, bf16[4,2,160,384]{3,2,1,0:T(8,128)(2,1)S(1)}, u32[]{:S(2)}, u32[]{:S(2)}) %collective-permute-start.20) | collective-permute-done | bytes 983072 | tf_op jit(solution)/shard_map/ppermute | solution.py:26
  278.0 2.0 fusion.1
  280.1 1.1 pad_maximum_fusion.1
  281.4 2.4 collective-permute-start.22
  283.8 0.8 pad_maximum_fusion.2
  284.6 1.8 collective-permute-start.23
  286.4 5.9 %shard_map.133 = bf16[16,16,5120]{2,1,0:T(8,128)(2,1)} custom-call(bf16[16,16,5120]{2,1,0:T(8,128)(2,1)} %copy-done.7), custom_call_target="tpu_custom_call" | custom-call | flops 3000000000 | bytes 9000000 | tf_op jit(solution)/shard_map/pallas_call | solution.py:310
  292.3 14.8 %collective-permute-done.22 = bf16[2,2,160,384]{3,2,1,0:T(8,128)(2,1)S(1)} collective-permute-done((bf16[2,2,160,384]{3,2,1,0:T(8,128)(2,1)}, bf16[2,2,160,384]{3,2,1,0:T(8,128)(2,1)S(1)}, u32[]{:S(2)}, u32[]{:S(2)}) %collective-permute-start.22) | collective-permute-done | bytes 491552 | tf_op jit(solution)/shard_map/ppermute | solution.py:26
  307.1 3.1 collective-permute-done.23
  310.1 1.0 fusion.7
  311.1 1.1 fusion.8
  313.0 3.4 %collective-permute-start.25 = (bf16[2,160,384]{2,1,0:T(8,128)(2,1)S(1)}, bf16[2,160,384]{2,1,0:T(8,128)(2,1)S(1)}, u32[]{:S(2)}, u32[]{:S(2)}) collective-permute-start(bf16[2,160,384]{2,1,0:T(8,128)(2,1)S(1)} %fusion.8), channel_id=1, source_target_pairs={{0,12},{1,13},{2,14},{3,15},{4,0},{5,1},{6,2},{7,3},{8,4},{9,5},{1... | collective-permute-start | bytes 737288 | tf_op jit(solution)/shard_map/ppermute | solution.py:26
  316.5 11.2 %collective-permute-done.24 = bf16[2,160,384]{2,1,0:T(8,128)(2,1)S(1)} collective-permute-done((bf16[2,160,384]{2,1,0:T(8,128)(2,1)S(1)}, bf16[2,160,384]{2,1,0:T(8,128)(2,1)S(1)}, u32[]{:S(2)}, u32[]{:S(2)}) %collective-permute-start.24) | collective-permute-done | bytes 245792 | tf_op jit(solution)/shard_map/ppermute | solution.py:26
  327.7 1.1 convert_add_fusion.6
  328.8 1.0 convert_add_fusion.4
  330.6 0.9 fusion.5
  331.5 1.5 copy.19
  (63 shorter events, 4.7 us)
Async XLA Ops:
  0.6 6.8 %copy-start.11 = (bf16[1,2,128,320]{2,3,1,0:T(8,128)(2,1)S(1)}, bf16[1,2,128,320]{2,3,1,0:T(8,128)(2,1)}, u32[]{:S(2)}) copy-start(bf16[1,2,128,320]{2,3,1,0:T(8,128)(2,1)} %param.19) | copy-start | bytes 491524
  0.6 6.8 %copy-start.6 = (bf16[1,2,320,256]{3,2,1,0:T(8,128)(2,1)S(1)}, bf16[1,2,320,256]{3,2,1,0:T(8,128)(2,1)}, u32[]{:S(2)}) copy-start(bf16[1,2,320,256]{3,2,1,0:T(8,128)(2,1)} %param.18) | copy-start | bytes 983044
  0.7 15.0 %copy-start.14 = (s32[16]{0:T(128)S(1)}, s32[16]{0:T(128)}, u32[]{:S(2)}) copy-start(s32[16]{0:T(128)} %param.14) | copy-start | bytes 196
  0.7 16.2 %copy-start.15 = (s32[1,1,8]{2,1,0:T(1,128)S(1)}, s32[1,1,8]{2,1,0:T(1,128)}, u32[]{:S(2)}) copy-start(s32[1,1,8]{2,1,0:T(1,128)} %param.16) | copy-start | bytes 100
  0.7 16.3 %copy-start.16 = (s32[1,1,8]{2,1,0:T(1,128)S(1)}, s32[1,1,8]{2,1,0:T(1,128)}, u32[]{:S(2)}) copy-start(s32[1,1,8]{2,1,0:T(1,128)} %param.15) | copy-start | bytes 100
  4.0 23.7 %collective-permute-start = (bf16[464,384]{1,0:T(8,128)(2,1)S(1)}, bf16[464,384]{1,0:T(8,128)(2,1)S(1)}, u32[]{:S(2)}, u32[]{:S(2)}) collective-permute-start(bf16[464,384]{1,0:T(8,128)(2,1)S(1)} %pad_maximum_fusion.3), channel_id=1, source_target_pairs={{0,4},{1,5},{2,6},{3,7},{4,8},{5,9},{6,10},{7,11},{8,12},{9,13},{1... | collective-permute-start | bytes 1069064 | tf_op jit(solution)/shard_map/ppermute | solution.py:26
  7.4 9.6 %collective-permute-start.5 = (bf16[176,384]{1,0:T(8,128)(2,1)S(1)}, bf16[176,384]{1,0:T(8,128)(2,1)S(1)}, u32[]{:S(2)}, u32[]{:S(2)}) collective-permute-start(bf16[176,384]{1,0:T(8,128)(2,1)S(1)} %fusion.11), channel_id=1, source_target_pairs={{0,2},{1,3},{2,0},{3,1},{4,6},{5,7},{6,4},{7,5},{8,10},{9,11},{10,... | collective-permute-start | bytes 405512 | tf_op jit(solution)/shard_map/ppermute | solution.py:26
  10.5 11.6 %collective-permute-start.4 = (bf16[176,384]{1,0:T(8,128)(2,1)S(1)}, bf16[176,384]{1,0:T(8,128)(2,1)S(1)}, u32[]{:S(2)}, u32[]{:S(2)}) collective-permute-start(bf16[176,384]{1,0:T(8,128)(2,1)S(1)} %fusion.11), channel_id=1, source_target_pairs={{0,3},{1,0},{2,1},{3,2},{4,7},{5,4},{6,5},{7,6},{8,11},{9,8},{10,9... | collective-permute-start | bytes 405512 | tf_op jit(solution)/shard_map/ppermute | solution.py:26
  11.7 12.4 %collective-permute-start.3 = (bf16[176,384]{1,0:T(8,128)(2,1)S(1)}, bf16[176,384]{1,0:T(8,128)(2,1)S(1)}, u32[]{:S(2)}, u32[]{:S(2)}) collective-permute-start(bf16[176,384]{1,0:T(8,128)(2,1)S(1)} %fusion.11), channel_id=1, source_target_pairs={{0,1},{1,2},{2,3},{3,0},{4,5},{5,6},{6,7},{7,4},{8,9},{9,10},{10,1... | collective-permute-start | bytes 405512 | tf_op jit(solution)/shard_map/ppermute | solution.py:26
  12.6 28.4 %collective-permute-start.1 = (bf16[464,384]{1,0:T(8,128)(2,1)S(1)}, bf16[464,384]{1,0:T(8,128)(2,1)S(1)}, u32[]{:S(2)}, u32[]{:S(2)}) collective-permute-start(bf16[464,384]{1,0:T(8,128)(2,1)S(1)} %pad_maximum_fusion.3), channel_id=1, source_target_pairs={{0,12},{1,13},{2,14},{3,15},{4,0},{5,1},{6,2},{7,3},{8,4},{9,5},{1... | collective-permute-start | bytes 1069064 | tf_op jit(solution)/shard_map/ppermute | solution.py:26
  17.0 37.9 %copy-start.13 = (s32[1,1,8]{2,1,0:T(1,128)S(1)}, s32[1,1,8]{2,1,0:T(1,128)}, u32[]{:S(2)}) copy-start(s32[1,1,8]{2,1,0:T(1,128)} %param.13) | copy-start | bytes 100
  17.1 24.6 %collective-permute-start.2 = (bf16[464,384]{1,0:T(8,128)(2,1)S(1)}, bf16[464,384]{1,0:T(8,128)(2,1)S(1)}, u32[]{:S(2)}, u32[]{:S(2)}) collective-permute-start(bf16[464,384]{1,0:T(8,128)(2,1)S(1)} %pad_maximum_fusion.3), channel_id=1, source_target_pairs={{0,8},{1,9},{2,10},{3,11},{4,12},{5,13},{6,14},{7,15},{8,0},{9,1},... | collective-permute-start | bytes 1069064 | tf_op jit(solution)/shard_map/ppermute | solution.py:26
  22.1 20.3 %collective-permute-start.6 = (s32[16]{0:T(128)S(1)}, s32[16]{0:T(128)S(1)}, u32[]{:S(2)}, u32[]{:S(2)}) collective-permute-start(s32[16]{0:T(128)S(1)} %select_reduce_fusion.1), channel_id=1, source_target_pairs={{0,16},{1,17},{2,18},{3,19},{4,20},{5,21},{6,22},{7,23},{8,24},{9,... | collective-permute-start | bytes 200 | tf_op jit(solution)/shard_map/ppermute | solution.py:26
  24.1 18.4 %collective-permute-start.7 = (s32[16]{0:T(128)S(1)}, s32[16]{0:T(128)S(1)}, u32[]{:S(2)}, u32[]{:S(2)}) collective-permute-start(s32[16]{0:T(128)S(1)} %select_reduce_fusion), channel_id=1, source_target_pairs={{16,0},{17,1},{18,2},{19,3},{20,4},{21,5},{22,6},{23,7},{24,8},{25... | collective-permute-start | bytes 200 | tf_op jit(solution)/shard_map/ppermute | solution.py:26
  42.5 41.9 %collective-permute-start.9 = (bf16[1856,384]{1,0:T(8,128)(2,1)}, bf16[1856,384]{1,0:T(8,128)(2,1)S(1)}, u32[]{:S(2)}, u32[]{:S(2)}) collective-permute-start(bf16[1856,384]{1,0:T(8,128)(2,1)} %constant_dynamic-update-slice_fusion.refs_0_), channel_id=1, source_target_pairs={{0,3},{1,0},{2,1},{3,2},{4,7},{5,4},{6,5},{7,6},{8,11},{9,8},{10,9... | collective-permute-start | bytes 4276232 | tf_op jit(solution)/shard_map/ppermute | solution.py:26
  44.8 41.7 %collective-permute-start.8 = (bf16[1856,384]{1,0:T(8,128)(2,1)}, bf16[1856,384]{1,0:T(8,128)(2,1)S(1)}, u32[]{:S(2)}, u32[]{:S(2)}) collective-permute-start(bf16[1856,384]{1,0:T(8,128)(2,1)} %constant_dynamic-update-slice_fusion.refs_0_), channel_id=1, source_target_pairs={{0,1},{1,2},{2,3},{3,0},{4,5},{5,6},{6,7},{7,4},{8,9},{9,10},{10,1... | collective-permute-start | bytes 4276232 | tf_op jit(solution)/shard_map/ppermute | solution.py:26
  44.8 29.2 %collective-permute-start.13 = (bf16[704,384]{1,0:T(8,128)(2,1)S(1)}, bf16[704,384]{1,0:T(8,128)(2,1)}, u32[]{:S(2)}, u32[]{:S(2)}) collective-permute-start(bf16[704,384]{1,0:T(8,128)(2,1)S(1)} %pad_maximum_fusion.refs_5_), channel_id=1, source_target_pairs={{0,12},{1,13},{2,14},{3,15},{4,0},{5,1},{6,2},{7,3},{8,4},{9,5},{1... | collective-permute-start | bytes 1622024 | tf_op jit(solution)/shard_map/ppermute | solution.py:26
  49.8 28.9 %collective-permute-start.12 = (bf16[704,384]{1,0:T(8,128)(2,1)S(1)}, bf16[704,384]{1,0:T(8,128)(2,1)}, u32[]{:S(2)}, u32[]{:S(2)}) collective-permute-start(bf16[704,384]{1,0:T(8,128)(2,1)S(1)} %pad_maximum_fusion.refs_5_), channel_id=1, source_target_pairs={{0,4},{1,5},{2,6},{3,7},{4,8},{5,9},{6,10},{7,11},{8,12},{9,13},{1... | collective-permute-start | bytes 1622024 | tf_op jit(solution)/shard_map/ppermute | solution.py:26
  75.7 14.1 %collective-permute-start.15 = (bf16[352,384]{1,0:T(8,128)(2,1)}, bf16[352,384]{1,0:T(8,128)(2,1)}, u32[]{:S(2)}, u32[]{:S(2)}) collective-permute-start(bf16[352,384]{1,0:T(8,128)(2,1)} %slice.115), channel_id=1, source_target_pairs={{0,12},{1,13},{2,14},{3,15},{4,0},{5,1},{6,2},{7,3},{8,4},{9,5},{1... | collective-permute-start | bytes 811016 | tf_op jit(solution)/shard_map/ppermute | solution.py:26
  80.5 8.0 %copy-start.12 = (bf16[1,1,8,16,5120]{4,3,2,1,0:T(8,128)(2,1)S(1)}, bf16[1,1,8,16,5120]{4,3,2,1,0:T(8,128)(2,1)}, u32[]{:S(2)}) copy-start(bf16[1,1,8,16,5120]{4,3,2,1,0:T(8,128)(2,1)} %param.12) | copy-start | bytes 3932164
  80.5 14.6 %collective-permute-start.14 = (bf16[352,384]{1,0:T(8,128)(2,1)}, bf16[352,384]{1,0:T(8,128)(2,1)}, u32[]{:S(2)}, u32[]{:S(2)}) collective-permute-start(bf16[352,384]{1,0:T(8,128)(2,1)} %slice.114), channel_id=1, source_target_pairs={{0,4},{1,5},{2,6},{3,7},{4,8},{5,9},{6,10},{7,11},{8,12},{9,13},{1... | collective-permute-start | bytes 811016 | tf_op jit(solution)/shard_map/ppermute | solution.py:26
  84.3 18.0 %copy-start = (bf16[1856,384]{1,0:T(8,128)(2,1)}, bf16[1856,384]{1,0:T(8,128)(2,1)S(1)}, u32[]{:S(2)}) copy-start(bf16[1856,384]{1,0:T(8,128)(2,1)S(1)} %collective-permute-done.9.refs_2_) | copy-start | bytes 4276228
  85.4 12.5 %collective-permute-start.11 = (bf16[928,384]{1,0:T(8,128)(2,1)}, bf16[928,384]{1,0:T(8,128)(2,1)}, u32[]{:S(2)}, u32[]{:S(2)}) collective-permute-start(bf16[928,384]{1,0:T(8,128)(2,1)} %slice.113), channel_id=1, source_target_pairs={{0,3},{1,0},{2,1},{3,2},{4,7},{5,4},{6,5},{7,6},{8,11},{9,8},{10,9... | collective-permute-start | bytes 2138120 | tf_op jit(solution)/shard_map/ppermute | solution.py:26
  86.5 15.8 %copy-start.1 = (bf16[1856,384]{1,0:T(8,128)(2,1)}, bf16[1856,384]{1,0:T(8,128)(2,1)S(1)}, u32[]{:S(2)}) copy-start(bf16[1856,384]{1,0:T(8,128)(2,1)S(1)} %collective-permute-done.8.refs_1_) | copy-start | bytes 4276228
  87.6 14.8 %copy-start.3 = (f32[1,2,5120]{2,1,0:T(2,128)S(1)}, f32[1,2,5120]{2,1,0:T(2,128)}, u32[]{:S(2)}) copy-start(f32[1,2,5120]{2,1,0:T(2,128)} %param.17) | copy-start | bytes 122884
  87.6 14.8 %collective-permute-start.10 = (bf16[928,384]{1,0:T(8,128)(2,1)}, bf16[928,384]{1,0:T(8,128)(2,1)}, u32[]{:S(2)}, u32[]{:S(2)}) collective-permute-start(bf16[928,384]{1,0:T(8,128)(2,1)} %slice.112), channel_id=1, source_target_pairs={{0,1},{1,2},{2,3},{3,0},{4,5},{5,6},{6,7},{7,4},{8,9},{9,10},{10,1... | collective-permute-start | bytes 2138120 | tf_op jit(solution)/shard_map/ppermute | solution.py:26
  102.4 1.3 copy-start.2
  113.9 18.9 %collective-permute-start.16 = (bf16[128,5120]{1,0:T(8,128)(2,1)S(1)}, bf16[128,5120]{1,0:T(8,128)(2,1)S(1)}, u32[]{:S(2)}, u32[]{:S(2)}) collective-permute-start(bf16[128,5120]{1,0:T(8,128)(2,1)S(1)} %shard_map.129), channel_id=1, source_target_pairs={{0,16},{1,17},{2,18},{3,19},{4,20},{5,21},{6,22},{7,23},{8,24},{9,... | collective-permute-start | bytes 3932168 | tf_op jit(solution)/shard_map/ppermute | solution.py:26
  135.2 80.2 %all-to-all-start = ((bf16[16,16,5120]{2,1,0:T(8,128)(2,1)}), bf16[16,16,5120]{2,1,0:T(8,128)(2,1)S(1)}, u32[]{:S(2)}, u32[]{:S(2)}) async-start(bf16[16,16,5120]{2,1,0:T(8,128)(2,1)} %shard_map.132), calls=%async_computation | async-start | bytes 5242880 | tf_op jit(solution)/shard_map/all_to_all | solution.py:301
  140.5 73.6 %collective-permute-start.18 = (bf16[2,4,2,160,384]{4,3,2,1,0:T(8,128)(2,1)}, bf16[2,4,2,160,384]{4,3,2,1,0:T(8,128)(2,1)S(1)}, u32[]{:S(2)}, u32[]{:S(2)}) collective-permute-start(bf16[2,4,2,160,384]{4,3,2,1,0:T(8,128)(2,1)} %get-tuple-element.41), channel_id=1, source_target_pairs={{0,1},{1,2},{2,3},{3,0},{4,5},{5,6},{6,7},{7,4},{8,9},{9,10},{10,1... | collective-permute-start | bytes 5898248 | tf_op jit(solution)/shard_map/ppermute | solution.py:26
  142.4 73.0 %collective-permute-start.19 = (bf16[2,4,2,160,384]{4,3,2,1,0:T(8,128)(2,1)}, bf16[2,4,2,160,384]{4,3,2,1,0:T(8,128)(2,1)}, u32[]{:S(2)}, u32[]{:S(2)}) collective-permute-start(bf16[2,4,2,160,384]{4,3,2,1,0:T(8,128)(2,1)} %get-tuple-element.42), channel_id=1, source_target_pairs={{0,3},{1,0},{2,1},{3,2},{4,7},{5,4},{6,5},{7,6},{8,11},{9,8},{10,9... | collective-permute-start | bytes 5898248 | tf_op jit(solution)/shard_map/ppermute | solution.py:26
  143.8 17.3 %collective-permute-start.17 = (bf16[128,5120]{1,0:T(8,128)(2,1)}, bf16[128,5120]{1,0:T(8,128)(2,1)S(1)}, u32[]{:S(2)}, u32[]{:S(2)}) collective-permute-start(bf16[128,5120]{1,0:T(8,128)(2,1)} %get-tuple-element.40), channel_id=1, source_target_pairs={{16,0},{17,1},{18,2},{19,3},{20,4},{21,5},{22,6},{23,7},{24,8},{25... | collective-permute-start | bytes 3932168 | tf_op jit(solution)/shard_map/ppermute | solution.py:26
  214.1 1.3 copy-start.8
  215.4 1.5 copy-start.7
  216.9 114.6 %all-to-all-start.1 = ((bf16[16,16,5120]{2,1,0:T(8,128)(2,1)}), bf16[16,16,5120]{2,1,0:T(8,128)(2,1)S(1)}, u32[]{:S(2)}, u32[]{:S(2)}) async-start(bf16[16,16,5120]{2,1,0:T(8,128)(2,1)} %shard_map.131), calls=%async_computation.1 | async-start | bytes 5242880 | tf_op jit(solution)/shard_map/all_to_all | solution.py:301
  225.2 52.8 %copy-start.9 = (bf16[2,4,2,160,384]{4,3,2,1,0:T(8,128)(2,1)S(1)}, bf16[2,4,2,160,384]{4,3,2,1,0:T(8,128)(2,1)}, u32[]{:S(2)}) copy-start(bf16[2,4,2,160,384]{4,3,2,1,0:T(8,128)(2,1)} %copy-done.8) | copy-start | bytes 5898244
  225.2 52.8 %copy-start.10 = (bf16[4,2,320,384]{3,2,1,0:T(8,128)(2,1)S(1)}, bf16[4,2,320,384]{3,2,1,0:T(8,128)(2,1)}, u32[]{:S(2)}) copy-start(bf16[4,2,320,384]{3,2,1,0:T(8,128)(2,1)} %get-tuple-element.33) | copy-start | bytes 5898244
  227.9 50.0 %collective-permute-start.20 = (bf16[4,2,160,384]{3,2,1,0:T(8,128)(2,1)S(1)}, bf16[4,2,160,384]{3,2,1,0:T(8,128)(2,1)S(1)}, u32[]{:S(2)}, u32[]{:S(2)}) collective-permute-start(bf16[4,2,160,384]{3,2,1,0:T(8,128)(2,1)S(1)} %get-tuple-element.46), channel_id=1, source_target_pairs={{0,1},{1,2},{2,3},{3,0},{4,5},{5,6},{6,7},{7,4},{8,9},{9,10},{10,1... | collective-permute-start | bytes 2949128 | tf_op jit(solution)/shard_map/ppermute | solution.py:26
  230.2 47.8 %collective-permute-start.21 = (bf16[4,2,160,384]{3,2,1,0:T(8,128)(2,1)S(1)}, bf16[4,2,160,384]{3,2,1,0:T(8,128)(2,1)S(1)}, u32[]{:S(2)}, u32[]{:S(2)}) collective-permute-start(bf16[4,2,160,384]{3,2,1,0:T(8,128)(2,1)S(1)} %get-tuple-element.47), channel_id=1, source_target_pairs={{0,3},{1,0},{2,1},{3,2},{4,7},{5,4},{6,5},{7,6},{8,11},{9,8},{10,9... | collective-permute-start | bytes 2949128 | tf_op jit(solution)/shard_map/ppermute | solution.py:26
  279.9 1.2 copy-start.4
  280.0 1.5 copy-start.5
  281.4 25.6 %collective-permute-start.22 = (bf16[2,2,160,384]{3,2,1,0:T(8,128)(2,1)}, bf16[2,2,160,384]{3,2,1,0:T(8,128)(2,1)S(1)}, u32[]{:S(2)}, u32[]{:S(2)}) collective-permute-start(bf16[2,2,160,384]{3,2,1,0:T(8,128)(2,1)} %pad_maximum_fusion.1), channel_id=1, source_target_pairs={{0,4},{1,5},{2,6},{3,7},{4,8},{5,9},{6,10},{7,11},{8,12},{9,13},{1... | collective-permute-start | bytes 1474568 | tf_op jit(solution)/shard_map/ppermute | solution.py:26
  284.6 25.5 %collective-permute-start.23 = (bf16[2,2,160,384]{3,2,1,0:T(8,128)(2,1)}, bf16[2,2,160,384]{3,2,1,0:T(8,128)(2,1)}, u32[]{:S(2)}, u32[]{:S(2)}) collective-permute-start(bf16[2,2,160,384]{3,2,1,0:T(8,128)(2,1)} %pad_maximum_fusion.2), channel_id=1, source_target_pairs={{0,12},{1,13},{2,14},{3,15},{4,0},{5,1},{6,2},{7,3},{8,4},{9,5},{1... | collective-permute-start | bytes 1474568 | tf_op jit(solution)/shard_map/ppermute | solution.py:26
  312.2 15.4 %collective-permute-start.24 = (bf16[2,160,384]{2,1,0:T(8,128)(2,1)S(1)}, bf16[2,160,384]{2,1,0:T(8,128)(2,1)S(1)}, u32[]{:S(2)}, u32[]{:S(2)}) collective-permute-start(bf16[2,160,384]{2,1,0:T(8,128)(2,1)S(1)} %fusion.7), channel_id=1, source_target_pairs={{0,4},{1,5},{2,6},{3,7},{4,8},{5,9},{6,10},{7,11},{8,12},{9,13},{1... | collective-permute-start | bytes 737288 | tf_op jit(solution)/shard_map/ppermute | solution.py:26
  313.0 15.8 %collective-permute-start.25 = (bf16[2,160,384]{2,1,0:T(8,128)(2,1)S(1)}, bf16[2,160,384]{2,1,0:T(8,128)(2,1)S(1)}, u32[]{:S(2)}, u32[]{:S(2)}) collective-permute-start(bf16[2,160,384]{2,1,0:T(8,128)(2,1)S(1)} %fusion.8), channel_id=1, source_target_pairs={{0,12},{1,13},{2,14},{3,15},{4,0},{5,1},{6,2},{7,3},{8,4},{9,5},{1... | collective-permute-start | bytes 737288 | tf_op jit(solution)/shard_map/ppermute | solution.py:26
